TPU v7x, 256 devices: a whole 4x4x8 slice. The times are simulated.
256 devices in a mesh: member: 8 (over x, core), region: 32 (over z, y).
Axes of the slice: x: 4, y: 4, z: 8, core: 2. Of those that a mesh axis runs over, the one named last changes fastest.
Arguments:
- background: bfloat16 [128, 4096, 512], P('member', 'region'), may hold values from -6 to 6
- obs_anom: bfloat16 [128, 131072], P('member', 'region'), may hold values from -6 to 6
- innovation: float32 [131072], P('region'), may hold values from -6 to 6
- obs_error: float32 [131072], P('region'), may hold values from 0.5 to 2
- send_index: int32 [32, 8, 32, 512], P('region'), may hold values from 0 to 4095
- block_index: int32 [32, 8, 16, 2048], P('region', 'member'), may hold values from 0 to 16383
- block_count: int32 [32, 8, 16], P('region', 'member'), may hold values from 1 to 2048, as said below
- taper_index: int32 [32, 8, 16, 2048], P('region', 'member'), may hold values from 0 to 63
Outputs:
- analysis: bfloat16 [128, 4096, 512], P('member', 'region')
Inputs may be any that keep to these rules, and one draw needn't show every extreme that they name: `send_index`: local observation numbers of the sending region. `block_index`: positions in the pool of 16384 observations that the column's device receives, region of anchor major. `block_count`: some column has exactly 2048 live observations in every draw; regions differ in their density of observations.
All inputs are finite; a program needn't handle non-finite values.
Results may differ from a plain program's by a relative error of at most 0.0065.
Values may be sent and summed in bfloat16 or wider, within the bound.
A program may use at most 128 MiB of HBM per device.

v0:
```python
import jax
import jax.numpy as jnp
from jax import lax
from jax.sharding import PartitionSpec as P

K = 128
SLOT = 512
NTAPER = 64
NS_ITERS = 6


HIGHEST_PREC = lax.Precision.HIGHEST


def taper_weights(taper_index, block_count):
    radius = 2.0 * (taper_index.astype(jnp.float32) + 0.5) / NTAPER
    inside_part = (
        1.0 - 5.0 / 3.0 * radius**2 + 0.625 * radius**3 + 0.5 * radius**4 - 0.25 * radius**5
    )
    outside_part = (
        4.0
        - 5.0 * radius
        + 5.0 / 3.0 * radius**2
        + 0.625 * radius**3
        - 0.5 * radius**4
        + radius**5 / 12.0
        - 2.0 / (3.0 * radius)
    )
    weight = jnp.maximum(jnp.where(radius < 1.0, inside_part, outside_part), 0.0)
    places = lax.broadcasted_iota(jnp.int32, taper_index.shape, taper_index.ndim - 1)
    return jnp.where(places < block_count[..., None], weight, 0.0)


def column_transforms(obs_rows, obs_dev, weights):
    members = obs_rows.shape[2]
    root_weight = jnp.sqrt(weights)
    local_rows = (root_weight[:, :, None] * obs_rows).astype(jnp.bfloat16)
    scaled_dev = root_weight * obs_dev
    identity = jnp.eye(members, dtype=jnp.float32)
    gram_mat = jnp.einsum(
        "bla,blc->bac", local_rows, local_rows, preferred_element_type=jnp.float32
    )
    gram_mat = gram_mat + (members - 1.0) * identity
    projected = jnp.einsum(
        "bla,bl->ba",
        local_rows,
        scaled_dev,
        precision=HIGHEST_PREC,
        preferred_element_type=jnp.float32,
    )
    frob_norm = jnp.sqrt(jnp.sum(gram_mat * gram_mat, axis=(1, 2)))
    iterate = gram_mat / frob_norm[:, None, None]
    inverse_root = jnp.broadcast_to(identity, gram_mat.shape)
    for sweep_num in range(NS_ITERS):
        factor = 1.5 * identity - 0.5 * jnp.einsum(
            "bij,bjk->bik", inverse_root, iterate, precision=HIGHEST_PREC
        )
        iterate = jnp.einsum("bij,bjk->bik", iterate, factor, precision=HIGHEST_PREC)
        inverse_root = jnp.einsum("bij,bjk->bik", factor, inverse_root, precision=HIGHEST_PREC)
    weights_mat = jnp.sqrt(members - 1.0) * inverse_root / jnp.sqrt(frob_norm)[:, None, None]
    half_step = jnp.einsum("bij,bj->bi", inverse_root, projected, precision=HIGHEST_PREC)
    mean_shift = (
        jnp.einsum("bij,bj->bi", inverse_root, half_step, precision=HIGHEST_PREC)
        / frob_norm[:, None]
    )
    return (weights_mat + mean_shift[:, :, None]).astype(jnp.bfloat16)


def analysis_block(ensemble, transform):
    mean_state = jnp.mean(ensemble.astype(jnp.float32), axis=0)
    anomalies = (ensemble - mean_state).astype(jnp.bfloat16)
    combined = jnp.einsum("jcv,cjk->kcv", anomalies, transform, preferred_element_type=jnp.float32)
    return (mean_state + combined).astype(jnp.bfloat16)


def shards(
    background, obs_anom, innovation, obs_error, send_index, block_index, block_count, taper_index
):
    scaled_rows = (obs_anom.T.astype(jnp.float32) / obs_error[:, None]).astype(jnp.bfloat16)
    dscaled = (innovation / obs_error).astype(jnp.bfloat16)
    member_pos = lax.axis_index("member")
    member_count = lax.axis_size("member")
    wanted = send_index[0]
    region_total = wanted.shape[1]
    slot_share = SLOT // member_count
    ens_send = jnp.take(scaled_rows, wanted, axis=0)
    own_slots = lax.dynamic_slice_in_dim(wanted, member_pos * slot_share, slot_share, 2)
    innov_send = dscaled[own_slots][..., None]
    pool_ens, pool_innov = (
        lax.all_to_all(
            lax.all_to_all(ens_send, "member", split_axis=0, concat_axis=3, tiled=True),
            "region",
            split_axis=1,
            concat_axis=2,
            tiled=True,
        ),
        lax.all_to_all(
            lax.all_to_all(innov_send, "member", split_axis=0, concat_axis=3, tiled=True),
            "region",
            split_axis=1,
            concat_axis=2,
            tiled=True,
        ),
    )
    pool_rows = pool_ens.reshape(-1, K)
    pool_dev = (
        pool_innov.reshape(region_total, slot_share, member_count).transpose(0, 2, 1).reshape(-1)
    )
    block_rows = block_index[0, 0]
    weights = taper_weights(taper_index[0, 0], block_count[0, 0])
    obs_rows = jnp.take(pool_rows, block_rows, axis=0)
    obs_dev = pool_dev[block_rows].astype(jnp.float32)
    transform = column_transforms(obs_rows, obs_dev, weights)
    gathered = lax.all_to_all(background, "member", split_axis=1, concat_axis=0, tiled=True)
    updated = analysis_block(gathered, transform)
    return lax.all_to_all(updated, "member", split_axis=0, concat_axis=1, tiled=True)


def solution(mesh):
    in_specs = (
        P("member", "region", None),
        P("member", "region"),
        P("region"),
        P("region"),
        P("region", None, None, None),
        P("region", "member", None, None),
        P("region", "member", None),
        P("region", "member", None, None),
    )
    out_specs = P("member", "region", None)
    return jax.shard_map(shards, mesh=mesh, in_specs=in_specs, out_specs=out_specs, check_vma=False)
```

profile of v0, /device:TPU:1, one launch (start us, length us, event | category | flops | bytes accessed | tf_op | source)
XLA Modules:
  0.0 1123.8 jit_solution(5727415797452938439)
XLA Ops:
  1.9 100.9 %gather_fusion.2 = bf16[16384]{0:T(1024)(128)(2,1)S(1)} fusion(bf16[4096]{0:T(1024)(128)(2,1)S(1)} %divide_convert_fusion.1, s32[16384]{0:T(1024)S(1)} %broadcast_clamp_fusion.2), kind=kCustom, calls=%fused_computation.2 | custom fusion | bytes 131072 | tf_op jit(solution)/shard_map/gather | solution.py:88
  103.6 6.5 all-to-all-start.3
  111.1 457.1 %gather_fusion = bf16[131072,16]{1,0:T(8,128)(2,1)} fusion(bf16[4096,16]{1,0:T(8,128)(2,1)S(1)} %copy.58, s32[131072]{0:T(1024)S(1)} %broadcast_clamp_fusion), kind=kCustom, calls=%fused_computation | custom fusion | bytes 8912896 | tf_op jit(solution)/shard_map/jit(_take)/gather | solution.py:86
  568.2 26.4 %copy.59 = bf16[8,32,512,16]{2,3,1,0:T(8,128)(2,1)} copy(bf16[8,32,512,16]{3,2,1,0:T(8,128)(2,1)} %bitcast.172) | data formatting | bytes 8388608 | tf_op jit(solution)/shard_map/jit(_take)/gather | solution.py:86
  595.5 10.5 all-to-all-start.4
  606.0 4.9 broadcast_select_fusion
  610.9 4.0 all-to-all-done.4
  614.9 6.0 all-to-all-start.1
  620.9 2.5 copy.57
  623.4 46.4 %all-to-all-done.1 = bf16[8,32,512,16]{2,3,1,0:T(8,128)(2,1)} async-done(((bf16[8,32,512,16]{2,3,1,0:T(8,128)(2,1)}), bf16[8,32,512,16]{2,3,1,0:T(8,128)(2,1)}, u32[]{:S(2)}, u32[]{:S(2)}) %all-to-all-start.1) | async-done | bytes 4194336 | tf_op jit(solution)/shard_map/all_to_all | solution.py:91
  669.8 4.4 all-to-all-start
  674.2 4.8 copy.60
  679.0 21.5 %all-to-all-done = bf16[16,128,512]{2,0,1:T(8,128)(2,1)S(1)} async-done(((bf16[16,128,512]{2,0,1:T(8,128)(2,1)}), bf16[16,128,512]{2,0,1:T(8,128)(2,1)S(1)}, u32[]{:S(2)}, u32[]{:S(2)}) %all-to-all-start) | async-done | bytes 2097184 | tf_op jit(solution)/shard_map/all_to_all | solution.py:114
  700.6 5.0 all-to-all-start.2
  706.0 201.3 %gather_fusion.3 = bf16[32768]{0:T(1024)(128)(2,1)S(1)} fusion(bf16[16384]{0:T(1024)(128)(2,1)S(1)} %reshape.218, s32[32768]{0:T(1024)S(1)} %broadcast_clamp_fusion.1), kind=kCustom, calls=%fused_computation.3 | custom fusion | bytes 262144 | tf_op jit(solution)/shard_map/gather | solution.py:112
  908.2 2.4 copy.67
  911.6 2.8 fusion.2
  914.4 6.5 copy.62
  920.9 112.9 %gather_fusion.1 = bf16[32768,128]{1,0:T(8,128)(2,1)} fusion(bf16[16384,128]{1,0:T(8,128)(2,1)} %bitcast.171, s32[32768]{0:T(1024)S(1)} %broadcast_clamp_fusion.1), kind=kCustom, calls=%fused_computation.1 | custom fusion | bytes 16908288 | tf_op jit(solution)/shard_map/jit(_take)/gather | solution.py:111
  1033.9 12.5 %copy.63 = bf16[16,2048,128]{1,2,0:T(8,128)(2,1)} copy(bf16[16,2048,128]{2,1,0:T(8,128)(2,1)} %bitcast.173) | data formatting | bytes 16777216 | tf_op jit(solution)/shard_map/jit(_take)/gather | solution.py:111
  1046.4 11.2 multiply_reduce_fusion
  1057.6 2.4 fusion.11
  1060.0 1.3 fusion.22
  1065.9 1.4 fusion.9
  1073.3 1.2 fusion.7
  1076.9 1.2 fusion.6
  1078.2 1.4 fusion.51
  1079.6 6.6 fusion.13
  1086.2 1.7 convolution_bitcast_fusion
  1087.9 1.7 fusion.52
  1092.1 30.0 %all_to_all.81 = bf16[128,16,512]{2,1,0:T(8,128)(2,1)S(1)} all-to-all(bf16[128,16,512]{2,1,0:T(8,128)(2,1)S(1)} %copy.69), channel_id=1, replica_groups=mesh['member'=8,'region'=32] {'member'}, dimensions={0} | all-to-all | bytes 4194304 | tf_op jit(solution)/shard_map/all_to_all | solution.py:116
  1122.1 1.5 copy.70
  (71 shorter events, 22.0 us)
Async XLA Ops:
  1.9 108.3 %copy-start = (s32[1,8,32,512]{3,2,1,0:T(8,128)S(1)}, s32[1,8,32,512]{3,2,1,0:T(8,128)}, u32[]{:S(2)}) copy-start(s32[1,8,32,512]{3,2,1,0:T(8,128)} %param.12) | copy-start | bytes 1572868
  1.9 108.6 %copy-start.4 = (bf16[16,4096]{1,0:T(8,128)(2,1)S(1)}, bf16[16,4096]{1,0:T(8,128)(2,1)}, u32[]{:S(2)}) copy-start(bf16[16,4096]{1,0:T(8,128)(2,1)} %param.9) | copy-start | bytes 393220
  1.9 108.6 %copy-start.5 = (f32[4096]{0:T(1024)S(1)}, f32[4096]{0:T(1024)}, u32[]{:S(2)}) copy-start(f32[4096]{0:T(1024)} %param.11) | copy-start | bytes 49156
  103.6 491.0 %all-to-all-start.3 = ((bf16[8,2,1024]{2,1,0:T(2,128)(2,1)}), bf16[8,2,1024]{2,1,0:T(2,128)(2,1)S(1)}, u32[]{:S(2)}, u32[]{:S(2)}) async-start(bf16[8,2,1024]{2,1,0:T(2,128)(2,1)} %reshape.265), calls=%async_computation.3 | async-start | bytes 65536 | tf_op jit(solution)/shard_map/all_to_all | solution.py:98
  595.5 19.4 %all-to-all-start.4 = ((bf16[32,2,256]{2,1,0:T(2,128)(2,1)}), bf16[32,2,256]{2,1,0:T(2,128)(2,1)S(1)}, u32[]{:S(2)}, u32[]{:S(2)}) async-start(bf16[32,2,256]{2,1,0:T(2,128)(2,1)} %reshape.267), calls=%async_computation.4 | async-start | bytes 65536 | tf_op jit(solution)/shard_map/all_to_all | solution.py:97
  610.9 10.0 copy-start.1
  614.9 54.9 %all-to-all-start.1 = ((bf16[8,32,512,16]{2,3,1,0:T(8,128)(2,1)}), bf16[8,32,512,16]{2,3,1,0:T(8,128)(2,1)}, u32[]{:S(2)}, u32[]{:S(2)}) async-start(bf16[8,32,512,16]{2,3,1,0:T(8,128)(2,1)} %broadcast_select_fusion), calls=%async_computation.1 | async-start | bytes 8388608 | tf_op jit(solution)/shard_map/all_to_all | solution.py:91
  669.8 30.7 %all-to-all-start = ((bf16[16,128,512]{2,0,1:T(8,128)(2,1)}), bf16[16,128,512]{2,0,1:T(8,128)(2,1)S(1)}, u32[]{:S(2)}, u32[]{:S(2)}) async-start(bf16[16,128,512]{2,0,1:T(8,128)(2,1)} %copy.57), calls=%async_computation | async-start | bytes 4194304 | tf_op jit(solution)/shard_map/all_to_all | solution.py:114
  700.6 5.0 copy-start.2
  700.6 213.9 %all-to-all-start.2 = ((bf16[1,32,512,128]{2,3,0,1:T(8,128)(2,1)}), bf16[1,32,512,128]{2,3,0,1:T(8,128)(2,1)}, u32[]{:S(2)}, u32[]{:S(2)}) async-start(bf16[1,32,512,128]{2,3,0,1:T(8,128)(2,1)} %bitcast.174), calls=%async_computation.2 | async-start | bytes 8388608 | tf_op jit(solution)/shard_map/all_to_all | solution.py:90
  706.0 201.4 %copy-start.3 = (s32[1,1,16,2048]{3,2,1,0:T(8,128)S(1)}, s32[1,1,16,2048]{3,2,1,0:T(8,128)}, u32[]{:S(2)}) copy-start(s32[1,1,16,2048]{3,2,1,0:T(8,128)} %param.15) | copy-start | bytes 393220
  706.0 201.4 %copy-start.6 = (s32[1,1,16]{2,1,0:T(1,128)S(1)}, s32[1,1,16]{2,1,0:T(1,128)}, u32[]{:S(2)}) copy-start(s32[1,1,16]{2,1,0:T(1,128)} %param.14) | copy-start | bytes 196
  1057.6 2.4 copy-start.7
  1073.3 6.3 slice-start
  1075.7 3.8 slice-start.1
where the time goes:
time: 1130 us; the launch traced here: 1120 us
  local copies, waits for them, and re-layouts  933 us (83%)
  waiting for transfers between devices  72 us (6%)
  matrix products  44.2 us (4%)
  starting transfers between devices  32.4 us (3%)
  blocking collectives  30 us (3%)
  other arithmetic  11.7 us (1%)
    gather x2, local copies, waits for them, and re-layouts, shards(): ens_send = jnp.take(scaled_rows, wanted, axis=0)  483 us
    gather x1, local copies, waits for them, and re-layouts, shards(): obs_dev = pool_dev[block_rows].astype(jnp.float32)  201 us
    gather x2, local copies, waits for them, and re-layouts, shards(): obs_rows = jnp.take(pool_rows, block_rows, axis=0)  125 us
    gather x1, local copies, waits for them, and re-layouts, shards(): innov_send = dscaled[own_slots][..., None]  101 us
    all_to_all x1, waiting for transfers between devices, shards(): lax.all_to_all(ens_send, 'member', split_axis=0, concat_axis=3, tiled=True)  46.4 us
    all_to_all x1, blocking collectives, shards(): lax.all_to_all(updated, 'member', split_axis=0, concat_axis=1, tiled=True)  30 us
  transfers between devices with their start and end apart: 5, of which 3 were waited for; matrix products, arithmetic and copies ran while one was open for 63% of the time, Pallas kernels for 0%

commit v1 on v0

v1 whole, which is shorter than its diff:
```python
import functools

import jax
import jax.numpy as jnp
from jax import lax
from jax.experimental import pallas as pl
from jax.experimental.pallas import tpu as pltpu
from jax.sharding import PartitionSpec as P

K = 128
SLOT = 512
NTAPER = 64
NS_ITERS = 6
LANES = 128
CGROUP = 4

NT = (((1,), (1,)), ((), ()))
VMEM_SPEC = pl.BlockSpec(memory_space=pltpu.VMEM)
SMEM_SPEC = pl.BlockSpec(memory_space=pltpu.SMEM)
PARAMS = pltpu.CompilerParams(vmem_limit_bytes=56 * 2**20)


def taper_weights(taper_index, block_count):
    radius = 2.0 * (taper_index.astype(jnp.float32) + 0.5) / NTAPER
    r2 = radius * radius
    r3 = r2 * radius
    r4 = r2 * r2
    r5 = r4 * radius
    inside_part = 1.0 - 5.0 / 3.0 * r2 + 0.625 * r3 + 0.5 * r4 - 0.25 * r5
    outside_part = (
        4.0 - 5.0 * radius + 5.0 / 3.0 * r2 + 0.625 * r3 - 0.5 * r4 + r5 / 12.0
        - 2.0 / (3.0 * radius)
    )
    weight = jnp.maximum(jnp.where(radius < 1.0, inside_part, outside_part), 0.0)
    places = lax.broadcasted_iota(jnp.int32, taper_index.shape, 1)
    return jnp.where(places < block_count, weight, 0.0)


def gather_kernel(idx_smem, idx_ref, obs_ref, err_ref, innov2_ref, err2_ref, out_ref, dev_ref,
                  table, rows):
    regions = idx_ref.shape[0]
    obs_count = obs_ref.shape[1]
    for q in range(obs_count // SLOT):
        cols = pl.ds(q * SLOT, SLOT)
        scaled = (obs_ref[:, cols].astype(jnp.float32) / err_ref[:, cols]).astype(jnp.bfloat16)
        table[cols, :] = scaled.astype(jnp.float32).T
    dscaled = (innov2_ref[...] / err2_ref[...]).astype(jnp.bfloat16)

    def block(r, _):
        base = r * SLOT

        def body(g, _):
            first = pl.multiple_of(g * 32, 32)
            for j in range(32):
                rows[pl.ds(first + j, 1), :] = table[pl.ds(idx_smem[base + first + j], 1), :]
            return 0

        lax.fori_loop(0, SLOT // 32, body, 0)
        out_ref[r] = rows[...].T.astype(jnp.bfloat16)
        dev_ref[r] = dev_pick(idx_ref[r], dscaled)
        return 0

    lax.fori_loop(0, regions, block, 0)


def dev_pick(idx, dscaled):
    low = lax.broadcasted_iota(jnp.int32, (LANES, SLOT), 0) == (idx & (LANES - 1))
    picked = jnp.dot(
        dscaled, low.astype(jnp.float32).astype(jnp.bfloat16), preferred_element_type=jnp.float32
    )
    high = lax.broadcasted_iota(jnp.int32, picked.shape, 0) == (idx >> 7)
    return jnp.sum(jnp.where(high, picked, 0.0), axis=0, keepdims=True)


def gather_blocks(wanted, obs_full, innovation, obs_error):
    regions = wanted.shape[0]
    obs_count = obs_full.shape[1]
    return pl.pallas_call(
        gather_kernel,
        out_shape=(
            jax.ShapeDtypeStruct((regions, K, SLOT), jnp.bfloat16),
            jax.ShapeDtypeStruct((regions, 1, SLOT), jnp.float32),
        ),
        in_specs=[SMEM_SPEC] + [VMEM_SPEC] * 5,
        out_specs=(VMEM_SPEC, VMEM_SPEC),
        scratch_shapes=[
            pltpu.VMEM((obs_count, K), jnp.float32),
            pltpu.VMEM((SLOT, K), jnp.float32),
        ],
        compiler_params=PARAMS,
        cost_estimate=pl.CostEstimate(flops=10**9, bytes_accessed=6 * 2**20, transcendentals=0),
    )(
        wanted.reshape(-1),
        wanted.reshape(regions, 1, SLOT),
        obs_full,
        obs_error.reshape(1, obs_count),
        innovation.reshape(-1, LANES),
        obs_error.reshape(-1, LANES),
    )


def split(x):
    high = x.astype(jnp.bfloat16)
    low = (x - high.astype(jnp.float32)).astype(jnp.bfloat16)
    return high, low


def dot3(a, b):
    ah, al = a
    bh, bl = b
    return jnp.dot(
        jnp.concatenate([ah, al, ah], axis=1),
        jnp.concatenate([bh, bh, bl], axis=0),
        preferred_element_type=jnp.float32,
    )


def scatter_weights(c, bidx_ref, rho, wmat):
    p = bidx_ref[c]
    weight = rho[c]
    count = p.shape[1]
    rows = lax.broadcasted_iota(jnp.int32, (LANES, count), 0)
    first = (rows == (p >> 7)).astype(jnp.float32).astype(jnp.bfloat16)
    high = weight.astype(jnp.bfloat16).astype(jnp.float32)
    hit = rows == (p & (LANES - 1))
    second = jnp.concatenate(
        [
            jnp.where(hit, high, 0.0).astype(jnp.bfloat16),
            jnp.where(hit, weight - high, 0.0).astype(jnp.bfloat16),
        ],
        axis=0,
    )
    both = lax.dot_general(first, second, NT, preferred_element_type=jnp.float32)
    wmat[c] = both[:, :LANES] + both[:, LANES:]


def gram_block(r, block, dev, wmat, weighted, right, acc):
    columns = wmat.shape[0]
    lead = SLOT // LANES
    values = block.astype(jnp.float32)
    right[0:K, :] = block
    first = lax.broadcasted_iota(jnp.int32, (16, SLOT), 0) == 0
    right[K : K + 16, :] = jnp.where(first, dev, 0.0).astype(jnp.bfloat16)
    for c in range(columns):
        for q in range(lead):
            lanes = slice(q * LANES, (q + 1) * LANES)
            w = wmat[c, pl.ds(r * lead + q, 1), :]
            weighted[c * K : (c + 1) * K, lanes] = (values[:, lanes] * w).astype(jnp.bfloat16)
    acc[...] += lax.dot_general(
        weighted[...], right[...], NT, preferred_element_type=jnp.float32
    )


def eye():
    shape = (K, K)
    same = lax.broadcasted_iota(jnp.int32, shape, 0) == lax.broadcasted_iota(jnp.int32, shape, 1)
    return same.astype(jnp.float32)


def transforms(grams):
    identity = eye()
    members = float(K)
    mats = [g[:, :K] + (members - 1.0) * identity for g in grams]
    norms = [jnp.sqrt(jnp.sum(m * m, axis=(0, 1), keepdims=True)) for m in mats]
    ys = [m / n for m, n in zip(mats, norms)]
    zs = [1.5 * identity - 0.5 * y for y in ys]
    ys = [dot3(split(z), split(y)) for z, y in zip(zs, ys)]
    for sweep in range(1, NS_ITERS):
        sy = [split(y) for y in ys]
        sz = [split(z) for z in zs]
        sf = [split(1.5 * identity - 0.5 * dot3(z, y)) for z, y in zip(sz, sy)]
        if sweep == NS_ITERS - 1:
            zs = [dot3(f, z) for f, z in zip(sf, sz)]
        else:
            both = [
                dot3(f, tuple(jnp.concatenate([a, b], axis=1) for a, b in zip(y, z)))
                for f, y, z in zip(sf, sy, sz)
            ]
            ys = [b[:, :K] for b in both]
            zs = [b[:, K:] for b in both]
    sz = [split(z) for z in zs]
    half = [dot3(z, split(g[:, K:])) for z, g in zip(sz, grams)]
    full = [dot3(z, split(h)) for z, h in zip(sz, half)]
    out = []
    for z, f, n in zip(zs, full, norms):
        out.append(jnp.sqrt(members - 1.0) * z / jnp.sqrt(n) + f[:, 0:1] / n)
    return out


def analyse(c, transform, bg_ref, out_ref):
    state = bg_ref[:, c].reshape(K, bg_ref.shape[3]).astype(jnp.float32)
    mean_state = jnp.sum(state, axis=0, keepdims=True) * (1.0 / K)
    anomalies = (state - mean_state).astype(jnp.bfloat16)
    combined = jnp.dot(
        transform.T.astype(jnp.bfloat16), anomalies, preferred_element_type=jnp.float32
    )
    result = (mean_state + combined).astype(jnp.bfloat16)
    out_ref[:, c] = result.reshape(out_ref.shape[0], out_ref.shape[2], out_ref.shape[3])


def column_kernel(pool_ref, dev_ref, bidx_ref, taper_ref, count_ref, bg_ref, out_ref,
                  wmat, rho, weighted, right, acc):
    columns = bidx_ref.shape[0]
    regions = pool_ref.shape[0]
    for c in range(columns):
        rho[c] = taper_weights(taper_ref[c], count_ref[c])
    lax.fori_loop(0, columns, lambda c, _: (scatter_weights(c, bidx_ref, rho, wmat), 0)[1], 0)
    acc[...] = jnp.zeros_like(acc)
    right[...] = jnp.zeros_like(right)

    def one_block(r, _):
        gram_block(r, pool_ref[r], dev_ref[r], wmat, weighted, right, acc)
        return 0

    lax.fori_loop(0, regions, one_block, 0)

    def group(g, _):
        first = g * CGROUP
        grams = [acc[pl.ds((first + i) * K, K), :] for i in range(CGROUP)]
        for i, t in enumerate(transforms(grams)):
            analyse(first + i, t, bg_ref, out_ref)
        return 0

    lax.fori_loop(0, columns // CGROUP, group, 0)


def analyse_columns(pool, dev, block_rows, taper_index, block_count, state):
    columns, places = block_rows.shape
    return pl.pallas_call(
        column_kernel,
        out_shape=jax.ShapeDtypeStruct(state.shape, jnp.bfloat16),
        in_specs=[VMEM_SPEC] * 4 + [SMEM_SPEC, VMEM_SPEC],
        out_specs=VMEM_SPEC,
        scratch_shapes=[
            pltpu.VMEM((columns, LANES, LANES), jnp.float32),
            pltpu.VMEM((columns, 1, places), jnp.float32),
            pltpu.VMEM((columns * K, SLOT), jnp.bfloat16),
            pltpu.VMEM((2 * K, SLOT), jnp.bfloat16),
            pltpu.VMEM((columns * K, 2 * K), jnp.float32),
        ],
        compiler_params=PARAMS,
        cost_estimate=pl.CostEstimate(
            flops=2 * 10**10, bytes_accessed=12 * 2**20, transcendentals=0
        ),
    )(
        pool,
        dev,
        block_rows.reshape(columns, 1, places),
        taper_index.reshape(columns, 1, places),
        block_count,
        state,
    )


def shards(
    background, obs_anom, innovation, obs_error, send_index, block_index, block_count, taper_index
):
    member_pos = lax.axis_index("member")
    member_count = lax.axis_size("member")
    own, columns_all, values = background.shape
    columns = columns_all // member_count
    wanted = lax.dynamic_index_in_dim(send_index[0], member_pos, 0, keepdims=False)
    obs_full = lax.all_gather(obs_anom, "member", axis=0, tiled=True)
    send, send_dev = gather_blocks(wanted, obs_full, innovation, obs_error)
    exchange = functools.partial(
        lax.all_to_all, axis_name="region", split_axis=0, concat_axis=0, tiled=True
    )
    pool = exchange(send)
    dev = exchange(send_dev)
    state = background.transpose(1, 0, 2).reshape(member_count, columns, own, values)
    trade = functools.partial(
        lax.all_to_all, axis_name="member", split_axis=0, concat_axis=0, tiled=True
    )
    state = trade(state)
    updated = analyse_columns(
        pool, dev, block_index[0, 0], taper_index[0, 0], block_count[0, 0], state
    )
    result = trade(updated)
    return result.reshape(columns_all, own, values).transpose(1, 0, 2)


def solution(mesh):
    in_specs = (
        P("member", "region", None),
        P("member", "region"),
        P("region"),
        P("region"),
        P("region", None, None, None),
        P("region", "member", None, None),
        P("region", "member", None),
        P("region", "member", None, None),
    )
    out_specs = P("member", "region", None)
    return jax.shard_map(shards, mesh=mesh, in_specs=in_specs, out_specs=out_specs, check_vma=False)
```

time: 1130 us -> 275 us (0.24)
  local copies, waits for them, and re-layouts: 933 us -> 9.37 us
  Pallas kernels: 0 us -> 72.8 us
  matrix products: 44.2 us -> 0 us
  waiting for transfers between devices: 72 us -> 114 us
  blocking collectives: 30 us -> 53.1 us
  starting transfers between devices: 32.4 us -> 11.7 us
  between operations: 0.76 us -> 13.4 us
  other arithmetic: 11.7 us -> 0 us
    gather x6 -> x0, local copies, waits for them, and re-layouts: 911 us -> none  [the longest x2 483 us: shards(): ens_send = jnp.take(scaled_rows, wanted, axis=0)]
    pallas_call x0 -> x2, Pallas kernels: none -> 72.8 us  [the longest x1 48.8 us: analyse_columns(): pl.pallas_call(column_kernel, out_shape=jax.ShapeDtypeStruct(state.shape,...]
    dot_general x22 -> x0, matrix products: 44.2 us -> none  [the longest x1 11.2 us: column_transforms(): jnp.einsum('bla,blc->bac', local_rows, local_rows, preferred_element_type...]
    all_to_all x1 -> x2, blocking collectives: 30 us -> 53.1 us  [the longest x1 34.5 us: shards(): result = trade(updated)]
    all_gather x0 -> x1, waiting for transfers between devices: none -> 22.5 us  [shards(): obs_full = lax.all_gather(obs_anom, 'member', axis=0, tiled=True)]
    all_to_all x5 -> x2, starting transfers between devices: 32.4 us -> 11.7 us  [the longest x1 6.75 us: shards(): state = trade(state)]
    all_to_all x5 -> x2, waiting for transfers between devices: 72 us -> 90.7 us  [the longest x1 90.7 us: shards(): pool = exchange(send)]
    all_to_all x5 -> x0, local copies, waits for them, and re-layouts: 12.9 us -> none  [the longest x1 6.5 us: shards(): lax.all_to_all(lax.all_to_all(ens_send, 'member', split_axis=0, concat_ax...]
  transfers between devices with their start and end apart: 5 -> 3, of which waited for: 3 -> 2; matrix products, arithmetic and copies ran while one was open for 63% -> 3% of each run, Pallas kernels for 0% -> 9%
where the time goes in v1:
time: 275 us; the launch traced here: 274 us
  waiting for transfers between devices  114 us (41%)
  Pallas kernels  72.8 us (26%)
  blocking collectives  53.1 us (19%)
  between operations  13.4 us (5%)
  starting transfers between devices  11.7 us (4%)
  local copies, waits for them, and re-layouts  9.37 us (3%)
    all_to_all x1, waiting for transfers between devices, shards(): pool = exchange(send)  90.7 us
    pallas_call x1, Pallas kernels, analyse_columns(): pl.pallas_call(column_kernel, out_shape=jax.ShapeDtypeStruct(state.shape,...  48.8 us
    all_to_all x1, blocking collectives, shards(): result = trade(updated)  34.5 us
    pallas_call x1, Pallas kernels, gather_blocks(): pl.pallas_call(gather_kernel, out_shape=(jax.ShapeDtypeStruct((regions, K...  24.1 us
    all_gather x1, waiting for transfers between devices, shards(): obs_full = lax.all_gather(obs_anom, 'member', axis=0, tiled=True)  22.5 us
    all_to_all x1, blocking collectives, shards(): dev = exchange(send_dev)  18.6 us
    all_to_all x1, starting transfers between devices, shards(): state = trade(state)  6.75 us
  transfers between devices with their start and end apart: 3, of which 2 were waited for; matrix products, arithmetic and copies ran while one was open for 3% of the time, Pallas kernels for 9%

profile of v1, /device:TPU:1, one launch (start us, length us, event | category | flops | bytes accessed | tf_op | source)
XLA Modules:
  0.0 274.5 jit_solution(4086694912356058942)
XLA Ops:
  6.5 0.0 copy-start
  6.5 0.0 all-gather.2.cloned.1.call-start
  6.5 0.7 all-gather.2.cloned.1.call-update
  7.3 4.1 %copy.9 = bf16[128,16,512]{2,1,0:T(8,128)(2,1)} copy(bf16[128,16,512]{2,0,1:T(8,128)(2,1)} %bitcast.20) | data formatting | bytes 4194304 | tf_op jit(solution)/shard_map/transpose | solution.py:270
  11.3 6.7 %all-to-all-start.2 = ((bf16[8,16,16,512]{3,2,1,0:T(8,128)(2,1)}), bf16[8,16,16,512]{3,2,1,0:T(8,128)(2,1)S(1)}, u32[]{:S(2)}, u32[]{:S(2)}) async-start(bf16[8,16,16,512]{3,2,1,0:T(8,128)(2,1)} %bitcast.5), calls=%async_computation.2 | async-start | bytes 4194304 | tf_op jit(solution)/shard_map/all_to_all | solution.py:274
  18.1 0.0 copy-done
  18.1 0.6 copy.11
  18.7 0.7 reshape.26.idx_ref
  19.4 22.5 %all-gather.2.cloned.1.call-done.obs_ref = bf16[128,4096]{1,0:T(8,128)(2,1)} async-done(((bf16[16,4096]{1,0:T(8,128)(2,1)}), bf16[128,4096]{1,0:T(8,128)(2,1)}) %all-gather.2.cloned.1.call-update) | async-done | bytes 1048592 | tf_op jit(solution)/shard_map/all_gather | solution.py:263
  41.9 24.1 %shard_map.82 = (bf16[32,128,512]{2,1,0:T(8,128)(2,1)}, f32[32,1,512]{2,1,0:T(1,128)}) custom-call(s32[16384]{0:T(1024)} %bitcast.21, s32[32,1,512]{2,1,0:T(1,128)} %reshape.26.idx_ref, bf16[128,4096]{1,0:T(8,128)(2,1)} %all-gather.2.cloned.1.call-done.obs_ref, f32[1,4096]{1,0:T(1,128)} %bitcast.22, f32[32,128]{1,0:T(8,128)} %bitcast.24, f32[32,128]{1,0:T(8,128)} %bitcast.23), custom_call_target="tpu_custom_call" | custom-call | flops 1000000000 | bytes 6291456 | tf_op jit(solution)/shard_map/pallas_call | solution.py:78
  66.0 0.0 all-to-all-done.2.bg_ref
  66.0 0.0 copy-start.1
  66.0 18.6 %all_to_all.20.dev_ref = f32[32,1,512]{2,1,0:T(1,128)} all-to-all(f32[32,1,512]{2,1,0:T(1,128)} %get-tuple-element.8), channel_id=1, replica_groups=mesh['member'=8,'region'=32] {'region'}, dimensions={0} | all-to-all | bytes 131072 | tf_op jit(solution)/shard_map/all_to_all | solution.py:269
  84.6 0.0 copy-start.2
  84.6 0.0 copy-start.3
  84.6 0.0 copy-done.1
  84.6 5.0 %all-to-all-start = ((bf16[32,128,512]{2,1,0:T(8,128)(2,1)}), bf16[32,128,512]{2,1,0:T(8,128)(2,1)}, u32[]{:S(2)}, u32[]{:S(2)}) async-start(bf16[32,128,512]{2,1,0:T(8,128)(2,1)} %get-tuple-element.7), calls=%async_computation | async-start | bytes 8388608 | tf_op jit(solution)/shard_map/all_to_all | solution.py:268
  89.6 0.0 copy-done.2
  89.6 0.7 reshape_squeeze.6.bidx_ref
  90.4 0.0 copy-done.3
  90.4 0.7 reshape_squeeze.7.taper_ref
  91.1 90.7 %all-to-all-done.pool_ref = bf16[32,128,512]{2,1,0:T(8,128)(2,1)} async-done(((bf16[32,128,512]{2,1,0:T(8,128)(2,1)}), bf16[32,128,512]{2,1,0:T(8,128)(2,1)}, u32[]{:S(2)}, u32[]{:S(2)}) %all-to-all-start) | async-done | bytes 4194336 | tf_op jit(solution)/shard_map/all_to_all | solution.py:268
  181.9 48.8 %shard_map.83 = bf16[8,16,16,512]{3,2,1,0:T(8,128)(2,1)} custom-call(bf16[32,128,512]{2,1,0:T(8,128)(2,1)} %all-to-all-done.pool_ref, f32[32,1,512]{2,1,0:T(1,128)} %all_to_all.20.dev_ref, s32[16,1,2048]{2,1,0:T(1,128)} %reshape_squeeze.6.bidx_ref, s32[16,1,2048]{2,1,0:T(1,128)} %reshape_squeeze.7.taper_ref, s32[16]{0:T(128)} %bitcast.25, ...), custom_call_target="tpu_custom_call" | custom-call | flops 20000000000 | bytes 12582912 | tf_op jit(solution)/shard_map/pallas_call | solution.py:229
  230.6 34.5 %all_to_all.21 = bf16[8,16,16,512]{3,2,1,0:T(8,128)(2,1)S(1)} all-to-all(bf16[8,16,16,512]{3,2,1,0:T(8,128)(2,1)} %shard_map.83), channel_id=1, replica_groups=mesh['member'=8,'region'=32] {'member'}, dimensions={0} | all-to-all | bytes 4194304 | tf_op jit(solution)/shard_map/all_to_all | solution.py:278
  265.1 2.5 copy.13
  (2 shorter events, 0.0 us)
Async XLA Ops:
  6.5 11.5 %copy-start = (s32[1,8,32,512]{3,2,1,0:T(8,128)S(1)}, s32[1,8,32,512]{3,2,1,0:T(8,128)}, u32[]{:S(2)}) copy-start(s32[1,8,32,512]{3,2,1,0:T(8,128)} %param.12) | copy-start | bytes 1572868
  6.5 35.4 %all-gather.2.cloned.1.call-start = ((), (), s32[]{:S(2)}) async-start(), calls=%async_computation.4 | async-start | bytes 1179648 | tf_op jit(solution)/shard_map/all_gather | solution.py:263
  11.3 54.7 %all-to-all-start.2 = ((bf16[8,16,16,512]{3,2,1,0:T(8,128)(2,1)}), bf16[8,16,16,512]{3,2,1,0:T(8,128)(2,1)S(1)}, u32[]{:S(2)}, u32[]{:S(2)}) async-start(bf16[8,16,16,512]{3,2,1,0:T(8,128)(2,1)} %bitcast.5), calls=%async_computation.2 | async-start | bytes 4194304 | tf_op jit(solution)/shard_map/all_to_all | solution.py:274
  66.0 18.6 %copy-start.1 = (bf16[8,16,16,512]{3,2,1,0:T(8,128)(2,1)}, bf16[8,16,16,512]{3,2,1,0:T(8,128)(2,1)S(1)}, u32[]{:S(2)}) copy-start(bf16[8,16,16,512]{3,2,1,0:T(8,128)(2,1)S(1)} %all-to-all-done.2.bg_ref) | copy-start | bytes 6291460
  84.6 5.0 %copy-start.2 = (s32[1,1,16,2048]{3,2,1,0:T(8,128)S(1)}, s32[1,1,16,2048]{3,2,1,0:T(8,128)}, u32[]{:S(2)}) copy-start(s32[1,1,16,2048]{3,2,1,0:T(8,128)} %param.13) | copy-start | bytes 393220
  84.6 5.8 %copy-start.3 = (s32[1,1,16,2048]{3,2,1,0:T(8,128)S(1)}, s32[1,1,16,2048]{3,2,1,0:T(8,128)}, u32[]{:S(2)}) copy-start(s32[1,1,16,2048]{3,2,1,0:T(8,128)} %param.15) | copy-start | bytes 393220
  84.6 97.2 %all-to-all-start = ((bf16[32,128,512]{2,1,0:T(8,128)(2,1)}), bf16[32,128,512]{2,1,0:T(8,128)(2,1)}, u32[]{:S(2)}, u32[]{:S(2)}) async-start(bf16[32,128,512]{2,1,0:T(8,128)(2,1)} %get-tuple-element.7), calls=%async_computation | async-start | bytes 8388608 | tf_op jit(solution)/shard_map/all_to_all | solution.py:268
Sparse Core Ops, SparseCore 0:
  9.2 32.6 all-gather.1

commit v2 on v1

v2 whole, which is shorter than its diff:
```python
import jax
import jax.numpy as jnp
from jax import lax
from jax.experimental import pallas as pl
from jax.experimental.pallas import tpu as pltpu
from jax.sharding import PartitionSpec as P

K = 128
SLOT = 512
NTAPER = 64
NS_ITERS = 6
LANES = 128
CGROUP = 4
MEMBERS = 8
REGIONS = 32
NZ = 8
NY = 4
BLOCKS = 30
MESH = pl.DeviceIdType.MESH

NT = (((1,), (1,)), ((), ()))
VMEM_SPEC = pl.BlockSpec(memory_space=pltpu.VMEM)
SMEM_SPEC = pl.BlockSpec(memory_space=pltpu.SMEM)


def taper_weights(taper_index, block_count):
    radius = 2.0 * (taper_index.astype(jnp.float32) + 0.5) / NTAPER
    r2 = radius * radius
    r3 = r2 * radius
    r4 = r2 * r2
    r5 = r4 * radius
    inside_part = 1.0 - 5.0 / 3.0 * r2 + 0.625 * r3 + 0.5 * r4 - 0.25 * r5
    outside_part = (
        4.0 - 5.0 * radius + 5.0 / 3.0 * r2 + 0.625 * r3 - 0.5 * r4 + r5 / 12.0
        - 2.0 / (3.0 * radius)
    )
    weight = jnp.maximum(jnp.where(radius < 1.0, inside_part, outside_part), 0.0)
    places = lax.broadcasted_iota(jnp.int32, taper_index.shape, 1)
    return jnp.where(places < block_count, weight, 0.0)


def dev_pick(idx, dscaled):
    low = lax.broadcasted_iota(jnp.int32, (LANES, SLOT), 0) == (idx & (LANES - 1))
    picked = jnp.dot(
        dscaled, low.astype(jnp.float32).astype(jnp.bfloat16), preferred_element_type=jnp.float32
    )
    high = lax.broadcasted_iota(jnp.int32, picked.shape, 0) == (idx >> 7)
    return jnp.sum(jnp.where(high, picked, 0.0), axis=0, keepdims=True)


def split(x):
    high = x.astype(jnp.bfloat16)
    low = (x - high.astype(jnp.float32)).astype(jnp.bfloat16)
    return high, low


def dot3(a, b):
    ah, al = a
    bh, bl = b
    return jnp.dot(
        jnp.concatenate([ah, al, ah], axis=1),
        jnp.concatenate([bh, bh, bl], axis=0),
        preferred_element_type=jnp.float32,
    )


def scatter_weights(c, bidx_ref, rho, wmat):
    p = bidx_ref[pl.ds(c, 1), :]
    weight = rho[pl.ds(c, 1), :]
    count = p.shape[1]
    rows = lax.broadcasted_iota(jnp.int32, (LANES, count), 0)
    first = (rows == (p >> 7)).astype(jnp.float32).astype(jnp.bfloat16)
    high = weight.astype(jnp.bfloat16).astype(jnp.float32)
    hit = rows == (p & (LANES - 1))
    second = jnp.concatenate(
        [
            jnp.where(hit, high, 0.0).astype(jnp.bfloat16),
            jnp.where(hit, weight - high, 0.0).astype(jnp.bfloat16),
        ],
        axis=0,
    )
    both = lax.dot_general(first, second, NT, preferred_element_type=jnp.float32)
    wmat[c] = both[:, :LANES] + both[:, LANES:]


def gram_block(r, block, dev, wmat, weighted, right, acc):
    columns = wmat.shape[0]
    lead = SLOT // LANES
    values = block.astype(jnp.float32)
    right[0:K, :] = block
    first = lax.broadcasted_iota(jnp.int32, (16, SLOT), 0) == 0
    right[K : K + 16, :] = jnp.where(first, dev, 0.0).astype(jnp.bfloat16)
    for c in range(columns):
        for q in range(lead):
            lanes = slice(q * LANES, (q + 1) * LANES)
            w = wmat[c, pl.ds(r * lead + q, 1), :]
            weighted[c * K : (c + 1) * K, lanes] = (values[:, lanes] * w).astype(jnp.bfloat16)
    acc[...] += lax.dot_general(
        weighted[...], right[...], NT, preferred_element_type=jnp.float32
    )


def eye():
    shape = (K, K)
    same = lax.broadcasted_iota(jnp.int32, shape, 0) == lax.broadcasted_iota(jnp.int32, shape, 1)
    return same.astype(jnp.float32)


def transforms(grams):
    identity = eye()
    members = float(K)
    mats = [g[:, :K] + (members - 1.0) * identity for g in grams]
    norms = [jnp.sqrt(jnp.sum(m * m, axis=(0, 1), keepdims=True)) for m in mats]
    ys = [m / n for m, n in zip(mats, norms)]
    zs = [1.5 * identity - 0.5 * y for y in ys]
    ys = [dot3(split(z), split(y)) for z, y in zip(zs, ys)]
    for sweep in range(1, NS_ITERS):
        sy = [split(y) for y in ys]
        sz = [split(z) for z in zs]
        sf = [split(1.5 * identity - 0.5 * dot3(z, y)) for z, y in zip(sz, sy)]
        if sweep == NS_ITERS - 1:
            zs = [dot3(f, z) for f, z in zip(sf, sz)]
        else:
            both = [
                dot3(f, tuple(jnp.concatenate([a, b], axis=1) for a, b in zip(y, z)))
                for f, y, z in zip(sf, sy, sz)
            ]
            ys = [b[:, :K] for b in both]
            zs = [b[:, K:] for b in both]
    sz = [split(z) for z in zs]
    half = [dot3(z, split(g[:, K:])) for z, g in zip(sz, grams)]
    full = [dot3(z, split(h)) for z, h in zip(sz, half)]
    out = []
    for z, f, n in zip(zs, full, norms):
        out.append(jnp.sqrt(members - 1.0) * z / jnp.sqrt(n) + f[:, 0:1] / n)
    return out


def analyse(c, transform, bg_ref, out_ref):
    state = bg_ref[:, c].reshape(K, bg_ref.shape[3]).astype(jnp.float32)
    mean_state = jnp.sum(state, axis=0, keepdims=True) * (1.0 / K)
    anomalies = (state - mean_state).astype(jnp.bfloat16)
    combined = jnp.dot(
        transform.T.astype(jnp.bfloat16), anomalies, preferred_element_type=jnp.float32
    )
    result = (mean_state + combined).astype(jnp.bfloat16)
    out_ref[:, c] = result.reshape(out_ref.shape[0], out_ref.shape[2], out_ref.shape[3])


def place(j):
    block = j + j // 24 + j // 27
    combo, dy = block // 4, block % 4
    distance = 2 - (combo + 2) // 4
    dz = distance * (1 - 2 * (combo % 2))
    slot = combo // 4 - combo // 7
    return slot, dz, dy


def region_at(z, y):
    return ((z + 16) % NZ) * NY + (y + 8) % NY


def kernel(idx_smem, idx_ref, obs_ref, err_ref, innov2_ref, err2_ref, bidx_ref, taper_ref,
           count_ref, bg_ref, out_ref,
           own, full, pair, dev2, table, rows, sent, sent_dev, pool, pool_dev, state, result,
           wmat, rho, weighted, right, acc,
           obs_send, obs_recv, pair_send, pair_recv, bg_send, bg_recv,
           pool_send, pool_recv, dev_send, dev_recv, out_send, out_recv):
    me = lax.axis_index("member")
    region = lax.axis_index("region")
    z, y = region // NY, region % NY
    partner = region_at(z + 4, y)
    columns = bidx_ref.shape[0]
    obs_count = obs_ref.shape[1]
    others = [lax.rem(me + k, MEMBERS) for k in range(1, MEMBERS)]

    barrier = pltpu.get_barrier_semaphore()
    for other in others:
        pl.semaphore_signal(barrier, inc=1, device_id={"member": other}, device_id_type=MESH)
    pl.semaphore_signal(barrier, inc=1, device_id={"region": partner}, device_id_type=MESH)
    near = [(dz, dy) for dz in (-2, -1, 0, 1, 2) for dy in range(NY) if (dz, dy) != (0, 0)]
    for dz, dy in near:
        pl.semaphore_signal(
            barrier, inc=1, device_id={"region": region_at(z + dz, y + dy)}, device_id_type=MESH
        )
    own[...] = (obs_ref[...].astype(jnp.float32) / err_ref[...]).astype(jnp.bfloat16)
    dev2[0] = (innov2_ref[...] / err2_ref[...]).astype(jnp.bfloat16)
    pl.semaphore_wait(barrier, len(others) + 1 + len(near))

    def remote(src, dst, send, recv, where):
        return pltpu.make_async_remote_copy(
            src_ref=src, dst_ref=dst, send_sem=send, recv_sem=recv,
            device_id=where, device_id_type=MESH,
        )

    def pair_copy():
        return remote(own, pair, pair_send.at[0], pair_recv.at[0], {"region": partner})

    def pair_dev_copy():
        return remote(dev2.at[0], dev2.at[1], pair_send.at[1], pair_recv.at[1],
                      {"region": partner})

    def obs_copy(src, slot, owner, to):
        return remote(src, full.at[slot, owner], obs_send.at[slot, to], obs_recv.at[slot, owner],
                      {"member": to})

    def bg_copy(owner, to):
        return remote(bg_ref.at[to], state.at[owner], bg_send.at[to], bg_recv.at[owner],
                      {"member": to})

    def block_copy(j, source, to):
        return remote(sent.at[j], pool.at[source], pool_send.at[j], pool_recv.at[source],
                      {"region": to})

    def block_dev_copy(j, source, to):
        return remote(sent_dev.at[j], pool_dev.at[source], dev_send.at[j], dev_recv.at[source],
                      {"region": to})

    def out_copy(g, owner, to):
        cols = pl.ds(g * CGROUP, CGROUP)
        return remote(result.at[to, cols], out_ref.at[owner, cols], out_send.at[g, to],
                      out_recv.at[g, owner], {"member": to})

    pair_copy().start()
    pair_dev_copy().start()
    for other in others:
        obs_copy(own, 0, me, other).start()
    full[0, me] = own[...]

    for c in range(columns):
        rho[pl.ds(c, 1), :] = taper_weights(taper_ref[pl.ds(c, 1), :], count_ref[c])
    half = columns // 2
    scatter = lambda c, _: (scatter_weights(c, bidx_ref, rho, wmat), 0)[1]
    lax.fori_loop(0, half, scatter, 0)
    acc[...] = jnp.zeros_like(acc)
    right[...] = jnp.zeros_like(right)

    pair_copy().wait_recv()
    for other in others:
        obs_copy(pair, 1, me, other).start()
    full[1, me] = pair[...]
    for other in others:
        bg_copy(me, other).start()
    keep_bg = pltpu.make_async_copy(bg_ref.at[me], state.at[me], bg_send.at[me])
    keep_bg.start()
    lax.fori_loop(half, columns, scatter, 0)
    pair_dev_copy().wait_recv()

    def build(slot):
        for other in others:
            obs_copy(own, slot, other, other).wait_recv()
        for q in range(obs_count // SLOT):
            part = full[slot, :, :, q * SLOT : (q + 1) * SLOT]
            part = part.reshape(K, SLOT).astype(jnp.float32)
            table[pl.ds(slot * obs_count + q * SLOT, SLOT), :] = part.T

    def gather(slot, to):
        base = (slot * REGIONS + to) * SLOT
        start = slot * obs_count

        def body(g, _):
            first = pl.multiple_of(g * 32, 32)
            for j in range(32):
                at = idx_smem[base + first + j] + start
                rows[pl.ds(first + j, 1), :] = table[pl.ds(at, 1), :]
            return 0

        lax.fori_loop(0, SLOT // 32, body, 0)
        picked = dev_pick(idx_ref[slot, pl.ds(to, 1), :], dev2[slot])
        return rows[...].T.astype(jnp.bfloat16), picked

    def send(j, _):
        slot, dz, dy = place(j)
        to = region_at(z + dz, y + dy)
        source = region_at(z + 4 * slot, y)
        block, dev = gather(slot, to)
        sent[j] = block
        sent_dev[j] = dev
        block_copy(j, source, to).start()
        block_dev_copy(j, source, to).start()
        return 0

    build(0)
    lax.fori_loop(0, 16, send, 0)
    build(1)
    lax.fori_loop(16, BLOCKS, send, 0)
    for slot in range(2):
        source = region_at(z + 4 * slot, y)
        block, dev = gather(slot, region)
        gram_block(source, block, dev, wmat, weighted, right, acc)

    def receive(j, _):
        slot, dz, dy = place(j)
        source = region_at(z - dz + 4 * slot, y - dy)
        block_copy(j, source, region).wait_recv()
        block_dev_copy(j, source, region).wait_recv()
        gram_block(source, pool[source], pool_dev[source], wmat, weighted, right, acc)
        return 0

    lax.fori_loop(0, BLOCKS, receive, 0)
    keep_bg.wait()
    for other in others:
        bg_copy(other, other).wait_recv()

    def group(g, _):
        first = g * CGROUP
        grams = [acc[pl.ds((first + i) * K, K), :] for i in range(CGROUP)]
        for i, t in enumerate(transforms(grams)):
            analyse(first + i, t, state, result)
        for other in others:
            out_copy(g, me, other).start()
        cols = pl.ds(first, CGROUP)
        pltpu.make_async_copy(result.at[me, cols], out_ref.at[me, cols], out_send.at[g, me]).start()
        return 0

    groups = columns // CGROUP
    lax.fori_loop(0, groups, group, 0)

    pair_copy().wait_send()
    pair_dev_copy().wait_send()
    for other in others:
        obs_copy(own, 0, me, other).wait_send()
        obs_copy(pair, 1, me, other).wait_send()
        bg_copy(me, other).wait_send()

    def drain(j, _):
        block_copy(j, region, region).wait_send()
        block_dev_copy(j, region, region).wait_send()
        return 0

    lax.fori_loop(0, BLOCKS, drain, 0)

    def finish(g, _):
        cols = pl.ds(g * CGROUP, CGROUP)
        for other in others:
            out_copy(g, me, other).wait_send()
            out_copy(g, other, other).wait_recv()
        pltpu.make_async_copy(result.at[me, cols], out_ref.at[me, cols], out_send.at[g, me]).wait()
        return 0

    lax.fori_loop(0, groups, finish, 0)


def assimilate(wanted, obs_anom, innovation, obs_error, block_rows, taper_index, block_count,
               state):
    columns, places = block_rows.shape
    own, obs_count = obs_anom.shape
    values = state.shape[3]
    groups = columns // CGROUP
    bf16, f32 = jnp.bfloat16, jnp.float32
    dma = pltpu.SemaphoreType.DMA
    return pl.pallas_call(
        kernel,
        out_shape=jax.ShapeDtypeStruct(state.shape, bf16),
        in_specs=[SMEM_SPEC] + [VMEM_SPEC] * 7 + [SMEM_SPEC, pl.BlockSpec(memory_space=pl.ANY)],
        out_specs=pl.BlockSpec(memory_space=pl.ANY),
        scratch_shapes=[
            pltpu.VMEM((own, obs_count), bf16),
            pltpu.VMEM((2, MEMBERS, own, obs_count), bf16),
            pltpu.VMEM((own, obs_count), bf16),
            pltpu.VMEM((2, obs_count // LANES, LANES), bf16),
            pltpu.VMEM((2 * obs_count, K), f32),
            pltpu.VMEM((SLOT, K), f32),
            pltpu.VMEM((BLOCKS, K, SLOT), bf16),
            pltpu.VMEM((BLOCKS, 1, SLOT), f32),
            pltpu.VMEM((REGIONS, K, SLOT), bf16),
            pltpu.VMEM((REGIONS, 1, SLOT), f32),
            pltpu.VMEM((MEMBERS, columns, own, values), bf16),
            pltpu.VMEM((MEMBERS, columns, own, values), bf16),
            pltpu.VMEM((columns, LANES, LANES), f32),
            pltpu.VMEM((columns, places), f32),
            pltpu.VMEM((columns * K, SLOT), bf16),
            pltpu.VMEM((2 * K, SLOT), bf16),
            pltpu.VMEM((columns * K, 2 * K), f32),
            dma((2, MEMBERS)),
            dma((2, MEMBERS)),
            dma((2,)),
            dma((2,)),
            dma((MEMBERS,)),
            dma((MEMBERS,)),
            dma((BLOCKS,)),
            dma((REGIONS,)),
            dma((BLOCKS,)),
            dma((REGIONS,)),
            dma((groups, MEMBERS)),
            dma((groups, MEMBERS)),
        ],
        compiler_params=pltpu.CompilerParams(
            vmem_limit_bytes=56 * 2**20, collective_id=0, has_side_effects=True
        ),
        cost_estimate=pl.CostEstimate(
            flops=2 * 10**10, bytes_accessed=12 * 2**20, transcendentals=0
        ),
    )(
        wanted.reshape(-1),
        wanted,
        obs_anom,
        obs_error.reshape(1, obs_count),
        innovation.reshape(-1, LANES),
        obs_error.reshape(-1, LANES),
        block_rows,
        taper_index,
        block_count,
        state,
    )


def shards(
    background, obs_anom, innovation, obs_error, send_index, block_index, block_count, taper_index
):
    own, columns_all, values = background.shape
    columns = columns_all // MEMBERS
    wanted = lax.dynamic_index_in_dim(send_index[0], lax.axis_index("member"), 0, keepdims=False)
    across = [(r, (r + REGIONS // 2) % REGIONS) for r in range(REGIONS)]
    wanted = jnp.stack([wanted, lax.ppermute(wanted, "region", across)])
    state = background.transpose(1, 0, 2).reshape(MEMBERS, columns, own, values)
    result = assimilate(
        wanted, obs_anom, innovation, obs_error, block_index[0, 0], taper_index[0, 0],
        block_count[0, 0], state,
    )
    return result.reshape(columns_all, own, values).transpose(1, 0, 2)


def solution(mesh):
    in_specs = (
        P("member", "region", None),
        P("member", "region"),
        P("region"),
        P("region"),
        P("region", None, None, None),
        P("region", "member", None, None),
        P("region", "member", None),
        P("region", "member", None, None),
    )
    out_specs = P("member", "region", None)
    return jax.shard_map(shards, mesh=mesh, in_specs=in_specs, out_specs=out_specs, check_vma=False)
```

time: 275 us -> 139 us (0.51)
  waiting for transfers between devices: 114 us -> 0.01 us
  blocking collectives: 53.1 us -> 0 us
  Pallas kernels: 72.8 us -> 119 us
  between operations: 13.4 us -> 0.03 us
  starting transfers between devices: 11.7 us -> 7.83 us
    all_to_all x2 -> x0, waiting for transfers between devices: 90.7 us -> none  [the longest x1 90.7 us: shards(): pool = exchange(send)]
    all_to_all x2 -> x0, blocking collectives: 53.1 us -> none  [the longest x1 34.5 us: shards(): result = trade(updated)]
    pallas_call x2 -> x1, Pallas kernels: 72.8 us -> 119 us  [assimilate(): pl.pallas_call(kernel, out_shape=jax.ShapeDtypeStruct(state.shape, bf16),...]
    all_gather x1 -> x0, waiting for transfers between devices: 22.5 us -> none  [shards(): obs_full = lax.all_gather(obs_anom, 'member', axis=0, tiled=True)]
    all_to_all x2 -> x0, starting transfers between devices: 11.7 us -> none  [the longest x1 6.75 us: shards(): state = trade(state)]
    ppermute x0 -> x1, starting transfers between devices: none -> 7.83 us  [shards(): wanted = jnp.stack([wanted, lax.ppermute(wanted, 'region', across)])]
  transfers between devices with their start and end apart: 3 -> 1, of which waited for: 2 -> 0; matrix products, arithmetic and copies ran while one was open for 3% -> 3% of each run, Pallas kernels for 9% -> 0%
where the time goes in v2:
time: 139 us; the launch traced here: 136 us
  Pallas kernels  119 us (86%)
  local copies, waits for them, and re-layouts  9.71 us (7%)
  starting transfers between devices  7.83 us (6%)
    pallas_call x1, Pallas kernels, assimilate(): pl.pallas_call(kernel, out_shape=jax.ShapeDtypeStruct(state.shape, bf16),...  119 us
    ppermute x1, starting transfers between devices, shards(): wanted = jnp.stack([wanted, lax.ppermute(wanted, 'region', across)])  7.83 us
    reshape x1, local copies, waits for them, and re-layouts, shards(): return result.reshape(columns_all, own, values).transpose(1, 0, 2)  4.07 us
    transpose x1, local copies, waits for them, and re-layouts, shards(): state = background.transpose(1, 0, 2).reshape(MEMBERS, columns, own, values)  4.07 us
  transfers between devices with their start and end apart: 1, of which 0 were waited for; matrix products, arithmetic and copies ran while one was open for 3% of the time, Pallas kernels for 0%

profile of v2, /device:TPU:1, one launch (start us, length us, event | category | flops | bytes accessed | tf_op | source)
XLA Modules:
  0.0 136.5 jit_solution(18361898872384752175)
XLA Ops:
  0.0 0.8 dynamic-slice_bitcast_fusion.1
  0.9 7.8 %collective-permute-start = (s32[32,512]{1,0:T(8,128)S(1)}, s32[32,512]{1,0:T(8,128)S(1)}, u32[]{:S(2)}, u32[]{:S(2)}) collective-permute-start(s32[32,512]{1,0:T(8,128)S(1)} %get-tuple-element.6), channel_id=1, source_target_pairs={{0,16},{1,17},{2,18},{3,19},{4,20},{5,21},{6,22},{7,23},{8,24},{9,... | collective-permute-start | bytes 196616 | tf_op jit(solution)/shard_map/ppermute | solution.py:415
  8.7 4.1 %copy.9 = bf16[128,16,512]{2,1,0:T(8,128)(2,1)} copy(bf16[128,16,512]{2,0,1:T(8,128)(2,1)} %bitcast.19) | data formatting | bytes 4194304 | tf_op jit(solution)/shard_map/transpose | solution.py:416
  12.7 0.0 collective-permute-done
  12.8 0.0 copy-start
  12.8 0.7 copy.11
  13.5 0.0 copy-done
  13.5 118.9 %shard_map.82 = bf16[8,16,16,512]{3,2,1,0:T(8,128)(2,1)} custom-call(s32[32768]{0:T(1024)} %bitcast.23, s32[2,32,512]{2,1,0:T(8,128)} %copy-done, bf16[16,4096]{1,0:T(8,128)(2,1)} %obs_ref.1, f32[1,4096]{1,0:T(1,128)} %bitcast.27, f32[32,128]{1,0:T(8,128)} %bitcast.29, f32[32,128]{1,0:T(8,128)} %bitcast.28, s32[16,2048]{1,0:T(8,128)} %bitcast.25, ...), custom_call_target="tpu_custom_call" | custom-call | flops 20000000000 | bytes 12582912 | tf_op jit(solution)/shard_map/pallas_call | solution.py:352
  132.4 4.1 %copy.13 = bf16[128,16,512]{2,0,1:T(8,128)(2,1)} copy(bf16[128,16,512]{2,1,0:T(8,128)(2,1)} %bitcast.21) | data formatting | bytes 4194304 | tf_op jit(solution)/shard_map/reshape | solution.py:421
  (1 shorter events, 0.0 us)
Async XLA Ops:
  0.9 11.9 %collective-permute-start = (s32[32,512]{1,0:T(8,128)S(1)}, s32[32,512]{1,0:T(8,128)S(1)}, u32[]{:S(2)}, u32[]{:S(2)}) collective-permute-start(s32[32,512]{1,0:T(8,128)S(1)} %get-tuple-element.6), channel_id=1, source_target_pairs={{0,16},{1,17},{2,18},{3,19},{4,20},{5,21},{6,22},{7,23},{8,24},{9,... | collective-permute-start | bytes 196616 | tf_op jit(solution)/shard_map/ppermute | solution.py:415
  12.8 0.7 copy-start

commit v3 on v2

--- a/solution.py
+++ b/solution.py
@@ -10,7 +10,8 @@
 NTAPER = 64
 NS_ITERS = 6
 LANES = 128
-CGROUP = 4
+CGROUP = 8
+OGROUP = 4
 MEMBERS = 8
 REGIONS = 32
 NZ = 8
@@ -83,21 +84,28 @@
     wmat[c] = both[:, :LANES] + both[:, LANES:]
 
 
-def gram_block(r, block, dev, wmat, weighted, right, acc):
+def gram_blocks(parts, wmat, right, acc):
     columns = wmat.shape[0]
     lead = SLOT // LANES
-    values = block.astype(jnp.float32)
-    right[0:K, :] = block
     first = lax.broadcasted_iota(jnp.int32, (16, SLOT), 0) == 0
-    right[K : K + 16, :] = jnp.where(first, dev, 0.0).astype(jnp.bfloat16)
-    for c in range(columns):
-        for q in range(lead):
-            lanes = slice(q * LANES, (q + 1) * LANES)
-            w = wmat[c, pl.ds(r * lead + q, 1), :]
-            weighted[c * K : (c + 1) * K, lanes] = (values[:, lanes] * w).astype(jnp.bfloat16)
-    acc[...] += lax.dot_general(
-        weighted[...], right[...], NT, preferred_element_type=jnp.float32
-    )
+    values = []
+    for b, (r, block, dev) in enumerate(parts):
+        lanes = slice(b * SLOT, (b + 1) * SLOT)
+        right[0:K, lanes] = block
+        right[K : K + 16, lanes] = jnp.where(first, dev, 0.0).astype(jnp.bfloat16)
+        values.append(block.astype(jnp.float32))
+    for c in range(0, columns, 2):
+        weighted = []
+        for column in (c, c + 1):
+            pieces = []
+            for v, (r, block, dev) in zip(values, parts):
+                for q in range(lead):
+                    w = wmat[column, pl.ds(r * lead + q, 1), :]
+                    pieces.append((v[:, q * LANES : (q + 1) * LANES] * w).astype(jnp.bfloat16))
+            weighted.append(jnp.concatenate(pieces, axis=1))
+        acc[:, c * K : (c + 2) * K] += lax.dot_general(
+            right[...], jnp.concatenate(weighted, axis=0), NT, preferred_element_type=jnp.float32
+        )
 
 
 def eye():
@@ -106,10 +114,10 @@
     return same.astype(jnp.float32)
 
 
-def transforms(grams):
+def transforms(grams, shifts):
     identity = eye()
     members = float(K)
-    mats = [g[:, :K] + (members - 1.0) * identity for g in grams]
+    mats = [g + (members - 1.0) * identity for g in grams]
     norms = [jnp.sqrt(jnp.sum(m * m, axis=(0, 1), keepdims=True)) for m in mats]
     ys = [m / n for m, n in zip(mats, norms)]
     zs = [1.5 * identity - 0.5 * y for y in ys]
@@ -128,11 +136,11 @@
             ys = [b[:, :K] for b in both]
             zs = [b[:, K:] for b in both]
     sz = [split(z) for z in zs]
-    half = [dot3(z, split(g[:, K:])) for z, g in zip(sz, grams)]
-    full = [dot3(z, split(h)) for z, h in zip(sz, half)]
+    half = [dot3(split(p), z) for z, p in zip(sz, shifts)]
+    full = [dot3(split(h), z) for z, h in zip(sz, half)]
     out = []
     for z, f, n in zip(zs, full, norms):
-        out.append(jnp.sqrt(members - 1.0) * z / jnp.sqrt(n) + f[:, 0:1] / n)
+        out.append(jnp.sqrt(members - 1.0) * z / jnp.sqrt(n) + f[0:1, :] / n)
     return out
 
 
@@ -141,15 +149,15 @@
     mean_state = jnp.sum(state, axis=0, keepdims=True) * (1.0 / K)
     anomalies = (state - mean_state).astype(jnp.bfloat16)
     combined = jnp.dot(
-        transform.T.astype(jnp.bfloat16), anomalies, preferred_element_type=jnp.float32
+        transform.astype(jnp.bfloat16), anomalies, preferred_element_type=jnp.float32
     )
     result = (mean_state + combined).astype(jnp.bfloat16)
     out_ref[:, c] = result.reshape(out_ref.shape[0], out_ref.shape[2], out_ref.shape[3])
 
 
 def place(j):
-    block = j + j // 24 + j // 27
-    combo, dy = block // 4, block % 4
+    block = j + 2 * (j // 24)
+    combo, dy = 2 * (block // 8) + block % 2, (block // 2) % 4
     distance = 2 - (combo + 2) // 4
     dz = distance * (1 - 2 * (combo % 2))
     slot = combo // 4 - combo // 7
@@ -160,11 +168,23 @@
     return ((z + 16) % NZ) * NY + (y + 8) % NY
 
 
-def kernel(idx_smem, idx_ref, obs_ref, err_ref, innov2_ref, err2_ref, bidx_ref, taper_ref,
+def permute_state(raw, state):
+    count = raw.shape[1] * raw.shape[2]
+    a = lax.broadcasted_iota(jnp.int32, (count, count), 0)
+    b = lax.broadcasted_iota(jnp.int32, (count, count), 1)
+    swap = (a // 16 == b % 16) & (a % 16 == b // 16)
+    swap = swap.astype(jnp.float32).astype(jnp.bfloat16)
+    for m in range(raw.shape[0]):
+        rows = raw[m].reshape(count, raw.shape[3])
+        moved = jnp.dot(swap, rows, preferred_element_type=jnp.float32).astype(jnp.bfloat16)
+        state[m] = moved.reshape(state.shape[1:])
+
+
+def kernel(send_ref, obs_ref, err_ref, innov2_ref, err2_ref, bidx_ref, taper_ref,
            count_ref, bg_ref, out_ref,
-           own, full, pair, dev2, table, rows, sent, sent_dev, pool, pool_dev, state, result,
-           wmat, rho, weighted, right, acc,
-           obs_send, obs_recv, pair_send, pair_recv, bg_send, bg_recv,
+           idx_smem, idx_ref, own, full, pair, dev2, table, sent, sent_dev, pool, pool_dev,
+           raw, state, result, wmat, rho, right, acc,
+           idx_sem, obs_send, obs_recv, forward_send, pair_send, pair_recv, bg_send, bg_recv,
            pool_send, pool_recv, dev_send, dev_recv, out_send, out_recv):
     me = lax.axis_index("member")
     region = lax.axis_index("region")
@@ -173,7 +193,14 @@
     columns = bidx_ref.shape[0]
     obs_count = obs_ref.shape[1]
     others = [lax.rem(me + k, MEMBERS) for k in range(1, MEMBERS)]
-
+    along = [lax.rem(me + k, MEMBERS) for k in range(2, MEMBERS, 2)]
+    beside = me + 1 - 2 * lax.rem(me, 2)
+    crossed = [lax.rem(beside + k, MEMBERS) for k in range(0, MEMBERS, 2)]
+
+    own_idx = pltpu.make_async_copy(send_ref.at[0, me], idx_ref.at[0], idx_sem.at[0])
+    own_idx.start()
+    own_smem = pltpu.make_async_copy(send_ref.at[0, me], idx_smem.at[0], idx_sem.at[1])
+    own_smem.start()
     barrier = pltpu.get_barrier_semaphore()
     for other in others:
         pl.semaphore_signal(barrier, inc=1, device_id={"member": other}, device_id_type=MESH)
@@ -200,12 +227,21 @@
         return remote(dev2.at[0], dev2.at[1], pair_send.at[1], pair_recv.at[1],
                       {"region": partner})
 
+    def pair_idx_copy():
+        return remote(send_ref.at[0, me], idx_ref.at[1], pair_send.at[2], pair_recv.at[2],
+                      {"region": partner})
+
+    def forward_copy(slot, owner):
+        return remote(full.at[slot, owner], full.at[slot, owner], forward_send.at[slot, owner],
+                      obs_recv.at[slot, owner], {"member": beside})
+
     def obs_copy(src, slot, owner, to):
         return remote(src, full.at[slot, owner], obs_send.at[slot, to], obs_recv.at[slot, owner],
                       {"member": to})
 
     def bg_copy(owner, to):
-        return remote(bg_ref.at[to], state.at[owner], bg_send.at[to], bg_recv.at[owner],
+        cols = pl.ds(pl.multiple_of(to * columns, columns), columns)
+        return remote(bg_ref.at[:, cols, :], raw.at[owner], bg_send.at[to], bg_recv.at[owner],
                       {"member": to})
 
     def block_copy(j, source, to):
@@ -217,37 +253,44 @@
                       {"region": to})
 
     def out_copy(g, owner, to):
-        cols = pl.ds(g * CGROUP, CGROUP)
+        cols = pl.ds(g * OGROUP, OGROUP)
         return remote(result.at[to, cols], out_ref.at[owner, cols], out_send.at[g, to],
                       out_recv.at[g, owner], {"member": to})
 
+    def spread(src, slot):
+        for other in along + [beside]:
+            obs_copy(src, slot, me, other).start()
+        full[slot, me] = src[...]
+
+    def forward(slot):
+        for other in along:
+            obs_copy(own, slot, other, other).wait_recv()
+            forward_copy(slot, other).start()
+
     pair_copy().start()
     pair_dev_copy().start()
-    for other in others:
-        obs_copy(own, 0, me, other).start()
-    full[0, me] = own[...]
+    pair_idx_copy().start()
+    spread(own, 0)
 
     for c in range(columns):
         rho[pl.ds(c, 1), :] = taper_weights(taper_ref[pl.ds(c, 1), :], count_ref[c])
-    half = columns // 2
-    scatter = lambda c, _: (scatter_weights(c, bidx_ref, rho, wmat), 0)[1]
-    lax.fori_loop(0, half, scatter, 0)
+
+    def scatter(i, _):
+        scatter_weights(2 * i, bidx_ref, rho, wmat)
+        scatter_weights(2 * i + 1, bidx_ref, rho, wmat)
+        return 0
+
+    lax.fori_loop(0, columns // 2, scatter, 0)
     acc[...] = jnp.zeros_like(acc)
-    right[...] = jnp.zeros_like(right)
-
+
+    forward(0)
     pair_copy().wait_recv()
-    for other in others:
-        obs_copy(pair, 1, me, other).start()
-    full[1, me] = pair[...]
-    for other in others:
-        bg_copy(me, other).start()
-    keep_bg = pltpu.make_async_copy(bg_ref.at[me], state.at[me], bg_send.at[me])
-    keep_bg.start()
-    lax.fori_loop(half, columns, scatter, 0)
-    pair_dev_copy().wait_recv()
+    spread(pair, 1)
+    own_idx.wait()
+    own_smem.wait()
 
     def build(slot):
-        for other in others:
+        for other in crossed:
             obs_copy(own, slot, other, other).wait_recv()
         for q in range(obs_count // SLOT):
             part = full[slot, :, :, q * SLOT : (q + 1) * SLOT]
@@ -255,19 +298,15 @@
             table[pl.ds(slot * obs_count + q * SLOT, SLOT), :] = part.T
 
     def gather(slot, to):
-        base = (slot * REGIONS + to) * SLOT
         start = slot * obs_count
-
-        def body(g, _):
-            first = pl.multiple_of(g * 32, 32)
-            for j in range(32):
-                at = idx_smem[base + first + j] + start
-                rows[pl.ds(first + j, 1), :] = table[pl.ds(at, 1), :]
-            return 0
-
-        lax.fori_loop(0, SLOT // 32, body, 0)
+        parts = []
+        for h in range(SLOT // LANES):
+            rows = [
+                table[pl.ds(idx_smem[slot, to, h * LANES + j] + start, 1), :] for j in range(LANES)
+            ]
+            parts.append(jnp.concatenate(rows, axis=0).T.astype(jnp.bfloat16))
         picked = dev_pick(idx_ref[slot, pl.ds(to, 1), :], dev2[slot])
-        return rows[...].T.astype(jnp.bfloat16), picked
+        return jnp.concatenate(parts, axis=1), picked
 
     def send(j, _):
         slot, dz, dy = place(j)
@@ -281,46 +320,88 @@
         return 0
 
     build(0)
-    lax.fori_loop(0, 16, send, 0)
+    lax.fori_loop(0, 8, send, 0)
+    forward(1)
+    lax.fori_loop(8, 16, send, 0)
+    pair_dev_copy().wait_recv()
+    pair_idx_copy().wait_recv()
+    pair_smem = pltpu.make_async_copy(idx_ref.at[1], idx_smem.at[1], idx_sem.at[0])
+    pair_smem.start()
+    for other in others:
+        bg_copy(me, other).start()
+    own_cols = pl.ds(pl.multiple_of(me * columns, columns), columns)
+    keep_bg = pltpu.make_async_copy(bg_ref.at[:, own_cols, :], raw.at[me], bg_send.at[me])
+    keep_bg.start()
     build(1)
+    pair_smem.wait()
     lax.fori_loop(16, BLOCKS, send, 0)
-    for slot in range(2):
+
+    def local(slot, _):
         source = region_at(z + 4 * slot, y)
         block, dev = gather(slot, region)
-        gram_block(source, block, dev, wmat, weighted, right, acc)
-
-    def receive(j, _):
-        slot, dz, dy = place(j)
-        source = region_at(z - dz + 4 * slot, y - dy)
-        block_copy(j, source, region).wait_recv()
-        block_dev_copy(j, source, region).wait_recv()
-        gram_block(source, pool[source], pool_dev[source], wmat, weighted, right, acc)
-        return 0
-
-    lax.fori_loop(0, BLOCKS, receive, 0)
+        pool[source] = block
+        pool_dev[source] = dev
+        return 0
+
+    lax.fori_loop(0, 2, local, 0)
+
+    def add(sources):
+        parts = [(source, pool[source], pool_dev[source]) for source in sources]
+        gram_blocks(parts, wmat, right, acc)
+
+    add([region, partner])
+
+    def receive(i, _):
+        sources = []
+        for j in (2 * i, 2 * i + 1):
+            slot, dz, dy = place(j)
+            source = region_at(z - dz + 4 * slot, y - dy)
+            block_copy(j, source, region).wait_recv()
+            block_dev_copy(j, source, region).wait_recv()
+            sources.append(source)
+        add(sources)
+        return 0
+
+    lax.fori_loop(0, 8, receive, 0)
     keep_bg.wait()
     for other in others:
         bg_copy(other, other).wait_recv()
-
-    def group(g, _):
-        first = g * CGROUP
-        grams = [acc[pl.ds((first + i) * K, K), :] for i in range(CGROUP)]
-        for i, t in enumerate(transforms(grams)):
-            analyse(first + i, t, state, result)
-        for other in others:
-            out_copy(g, me, other).start()
-        cols = pl.ds(first, CGROUP)
-        pltpu.make_async_copy(result.at[me, cols], out_ref.at[me, cols], out_send.at[g, me]).start()
-        return 0
-
-    groups = columns // CGROUP
-    lax.fori_loop(0, groups, group, 0)
+    permute_state(raw, state)
+    lax.fori_loop(8, BLOCKS // 2, receive, 0)
+
+    def own_out(g):
+        cols = pl.ds(g * OGROUP, OGROUP)
+        return pltpu.make_async_copy(result.at[me, cols], out_ref.at[me, cols], out_send.at[g, me])
+
+    def group(i, _):
+        first = i * CGROUP
+        where = [pl.ds(pl.multiple_of((first + k) * K, K), K) for k in range(CGROUP)]
+        grams = [acc[0:K, w] for w in where]
+        shifts = [acc[K : K + 16, w] for w in where]
+        done = transforms(grams, shifts)
+        for h in range(CGROUP // OGROUP):
+            g = i * (CGROUP // OGROUP) + h
+            for k in range(OGROUP):
+                at = h * OGROUP + k
+                analyse(first + at, done[at], state, result)
+            for other in others:
+                out_copy(g, me, other).start()
+            own_out(g).start()
+        return 0
+
+    groups = columns // OGROUP
+    lax.fori_loop(0, columns // CGROUP, group, 0)
 
     pair_copy().wait_send()
     pair_dev_copy().wait_send()
-    for other in others:
+    pair_idx_copy().wait_send()
+    for other in along + [beside]:
         obs_copy(own, 0, me, other).wait_send()
         obs_copy(pair, 1, me, other).wait_send()
+    for other in along:
+        forward_copy(0, other).wait_send()
+        forward_copy(1, other).wait_send()
+    for other in others:
         bg_copy(me, other).wait_send()
 
     def drain(j, _):
@@ -331,51 +412,54 @@
     lax.fori_loop(0, BLOCKS, drain, 0)
 
     def finish(g, _):
-        cols = pl.ds(g * CGROUP, CGROUP)
         for other in others:
             out_copy(g, me, other).wait_send()
             out_copy(g, other, other).wait_recv()
-        pltpu.make_async_copy(result.at[me, cols], out_ref.at[me, cols], out_send.at[g, me]).wait()
+        own_out(g).wait()
         return 0
 
     lax.fori_loop(0, groups, finish, 0)
 
 
-def assimilate(wanted, obs_anom, innovation, obs_error, block_rows, taper_index, block_count,
-               state):
+def assimilate(send_index, obs_anom, innovation, obs_error, block_rows, taper_index, block_count,
+               background):
     columns, places = block_rows.shape
     own, obs_count = obs_anom.shape
-    values = state.shape[3]
-    groups = columns // CGROUP
+    values = background.shape[2]
+    groups = columns // OGROUP
     bf16, f32 = jnp.bfloat16, jnp.float32
     dma = pltpu.SemaphoreType.DMA
+    anywhere = pl.BlockSpec(memory_space=pl.ANY)
     return pl.pallas_call(
         kernel,
-        out_shape=jax.ShapeDtypeStruct(state.shape, bf16),
-        in_specs=[SMEM_SPEC] + [VMEM_SPEC] * 7 + [SMEM_SPEC, pl.BlockSpec(memory_space=pl.ANY)],
-        out_specs=pl.BlockSpec(memory_space=pl.ANY),
+        out_shape=jax.ShapeDtypeStruct((MEMBERS, columns, own, values), bf16),
+        in_specs=[anywhere] + [VMEM_SPEC] * 6 + [SMEM_SPEC, anywhere],
+        out_specs=anywhere,
         scratch_shapes=[
+            pltpu.SMEM((2, REGIONS, SLOT), jnp.int32),
+            pltpu.VMEM((2, REGIONS, SLOT), jnp.int32),
             pltpu.VMEM((own, obs_count), bf16),
             pltpu.VMEM((2, MEMBERS, own, obs_count), bf16),
             pltpu.VMEM((own, obs_count), bf16),
             pltpu.VMEM((2, obs_count // LANES, LANES), bf16),
             pltpu.VMEM((2 * obs_count, K), f32),
-            pltpu.VMEM((SLOT, K), f32),
             pltpu.VMEM((BLOCKS, K, SLOT), bf16),
             pltpu.VMEM((BLOCKS, 1, SLOT), f32),
             pltpu.VMEM((REGIONS, K, SLOT), bf16),
             pltpu.VMEM((REGIONS, 1, SLOT), f32),
+            pltpu.VMEM((MEMBERS, own, columns, values), bf16),
             pltpu.VMEM((MEMBERS, columns, own, values), bf16),
             pltpu.VMEM((MEMBERS, columns, own, values), bf16),
             pltpu.VMEM((columns, LANES, LANES), f32),
             pltpu.VMEM((columns, places), f32),
-            pltpu.VMEM((columns * K, SLOT), bf16),
-            pltpu.VMEM((2 * K, SLOT), bf16),
-            pltpu.VMEM((columns * K, 2 * K), f32),
+            pltpu.VMEM((K + 16, 2 * SLOT), bf16),
+            pltpu.VMEM((K + 16, columns * K), f32),
+            dma((2,)),
             dma((2, MEMBERS)),
             dma((2, MEMBERS)),
-            dma((2,)),
-            dma((2,)),
+            dma((2, MEMBERS)),
+            dma((3,)),
+            dma((3,)),
             dma((MEMBERS,)),
             dma((MEMBERS,)),
             dma((BLOCKS,)),
@@ -392,8 +476,7 @@
             flops=2 * 10**10, bytes_accessed=12 * 2**20, transcendentals=0
         ),
     )(
-        wanted.reshape(-1),
-        wanted,
+        send_index,
         obs_anom,
         obs_error.reshape(1, obs_count),
         innovation.reshape(-1, LANES),
@@ -401,7 +484,7 @@
         block_rows,
         taper_index,
         block_count,
-        state,
+        background,
     )
 
 
@@ -409,14 +492,9 @@
     background, obs_anom, innovation, obs_error, send_index, block_index, block_count, taper_index
 ):
     own, columns_all, values = background.shape
-    columns = columns_all // MEMBERS
-    wanted = lax.dynamic_index_in_dim(send_index[0], lax.axis_index("member"), 0, keepdims=False)
-    across = [(r, (r + REGIONS // 2) % REGIONS) for r in range(REGIONS)]
-    wanted = jnp.stack([wanted, lax.ppermute(wanted, "region", across)])
-    state = background.transpose(1, 0, 2).reshape(MEMBERS, columns, own, values)
     result = assimilate(
-        wanted, obs_anom, innovation, obs_error, block_index[0, 0], taper_index[0, 0],
-        block_count[0, 0], state,
+        send_index, obs_anom, innovation, obs_error, block_index[0, 0], taper_index[0, 0],
+        block_count[0, 0], background,
     )
     return result.reshape(columns_all, own, values).transpose(1, 0, 2)
 

time: 139 us -> 121 us (0.87)
  starting transfers between devices: 7.83 us -> 0 us
  local copies, waits for them, and re-layouts: 9.71 us -> 4.07 us
  Pallas kernels: 119 us -> 115 us
    ppermute x1 -> x0, starting transfers between devices: 7.83 us -> none  [shards(): wanted = jnp.stack([wanted, lax.ppermute(wanted, 'region', across)])]
    transpose x1 -> x0, local copies, waits for them, and re-layouts: 4.07 us -> none  [shards(): state = background.transpose(1, 0, 2).reshape(MEMBERS, columns, own, values)]
    pallas_call x1, Pallas kernels: 119 us -> 115 us  [assimilate(): pl.pallas_call(kernel, out_shape=jax.ShapeDtypeStruct((MEMBERS, columns,...]
  transfers between devices with their start and end apart: 1 -> 0, of which waited for: 0 -> 0; matrix products, arithmetic and copies ran while one was open for 3% -> 0% of each run, Pallas kernels for 0% -> 0%
where the time goes in v3:
time: 121 us; the launch traced here: 120 us
  Pallas kernels  115 us (95%)
  local copies, waits for them, and re-layouts  4.07 us (3%)
    pallas_call x1, Pallas kernels, assimilate(): pl.pallas_call(kernel, out_shape=jax.ShapeDtypeStruct((MEMBERS, columns,...  115 us
    reshape x1, local copies, waits for them, and re-layouts, shards(): return result.reshape(columns_all, own, values).transpose(1, 0, 2)  4.07 us

profile of v3, /device:TPU:1, one launch (start us, length us, event | category | flops | bytes accessed | tf_op | source)
XLA Modules:
  0.0 119.5 jit_solution(5626234192815790990)
XLA Ops:
  0.0 115.4 %shard_map.82 = bf16[8,16,16,512]{3,2,1,0:T(8,128)(2,1)} custom-call(s32[1,8,32,512]{3,2,1,0:T(8,128)} %send_ref.1, bf16[16,4096]{1,0:T(8,128)(2,1)} %obs_ref.1, f32[1,4096]{1,0:T(1,128)} %bitcast.13, f32[32,128]{1,0:T(8,128)} %bitcast.15, f32[32,128]{1,0:T(8,128)} %bitcast.14, s32[16,2048]{1,0:T(8,128)} %bitcast.11, s32[16,2048]{1,0:T(8,128)} %bitcast.12, ...), custom_call_target="tpu_custom_call" | custom-call | flops 20000000000 | bytes 12582912 | tf_op jit(solution)/shard_map/pallas_call | solution.py:433
  115.5 4.1 %copy.11 = bf16[128,16,512]{2,0,1:T(8,128)(2,1)} copy(bf16[128,16,512]{2,1,0:T(8,128)(2,1)} %bitcast.10) | data formatting | bytes 4194304 | tf_op jit(solution)/shard_map/reshape | solution.py:499

commit v4 on v3

--- a/solution.py
+++ b/solution.py
@@ -10,8 +10,9 @@
 NTAPER = 64
 NS_ITERS = 6
 LANES = 128
-CGROUP = 8
+CGROUP = 4
 OGROUP = 4
+RESTORE_STEPS = 4
 MEMBERS = 8
 REGIONS = 32
 NZ = 8
@@ -168,16 +169,43 @@
     return ((z + 16) % NZ) * NY + (y + 8) % NY
 
 
-def permute_state(raw, state):
-    count = raw.shape[1] * raw.shape[2]
+def swap_matrix(count):
     a = lax.broadcasted_iota(jnp.int32, (count, count), 0)
     b = lax.broadcasted_iota(jnp.int32, (count, count), 1)
     swap = (a // 16 == b % 16) & (a % 16 == b // 16)
-    swap = swap.astype(jnp.float32).astype(jnp.bfloat16)
+    return swap.astype(jnp.float32).astype(jnp.bfloat16)
+
+
+def swap_block(swap, block):
+    rows = block.reshape(swap.shape[0], block.shape[2])
+    moved = jnp.dot(swap, rows, preferred_element_type=jnp.float32).astype(jnp.bfloat16)
+    return moved.reshape(block.shape)
+
+
+def permute_state(raw, state):
+    swap = swap_matrix(raw.shape[1] * raw.shape[2])
     for m in range(raw.shape[0]):
-        rows = raw[m].reshape(count, raw.shape[3])
-        moved = jnp.dot(swap, rows, preferred_element_type=jnp.float32).astype(jnp.bfloat16)
-        state[m] = moved.reshape(state.shape[1:])
+        state[m] = swap_block(swap, raw[m])
+
+
+def restore_kernel(blocks_ref, out_ref):
+    columns, own = blocks_ref.shape[1:3]
+    swap = swap_matrix(columns * own)
+    for m in range(blocks_ref.shape[0]):
+        out_ref[:, m * columns : (m + 1) * columns, :] = swap_block(swap, blocks_ref[m])
+
+
+def restore(blocks):
+    members, columns, own, values = blocks.shape
+    step = members // RESTORE_STEPS
+    return pl.pallas_call(
+        restore_kernel,
+        grid=(RESTORE_STEPS,),
+        out_shape=jax.ShapeDtypeStruct((own, members * columns, values), blocks.dtype),
+        in_specs=[pl.BlockSpec((step, columns, own, values), lambda i: (i, 0, 0, 0))],
+        out_specs=pl.BlockSpec((own, step * columns, values), lambda i: (0, i, 0)),
+        compiler_params=pltpu.CompilerParams(vmem_limit_bytes=60 * 2**20),
+    )(blocks)
 
 
 def kernel(send_ref, obs_ref, err_ref, innov2_ref, err2_ref, bidx_ref, taper_ref,
@@ -491,12 +519,11 @@
 def shards(
     background, obs_anom, innovation, obs_error, send_index, block_index, block_count, taper_index
 ):
-    own, columns_all, values = background.shape
     result = assimilate(
         send_index, obs_anom, innovation, obs_error, block_index[0, 0], taper_index[0, 0],
         block_count[0, 0], background,
     )
-    return result.reshape(columns_all, own, values).transpose(1, 0, 2)
+    return restore(result)
 
 
 def solution(mesh):

time: 121 us -> 120 us (level)
  local copies, waits for them, and re-layouts: 4.07 us -> 0 us
  Pallas kernels: 115 us -> 119 us
    pallas_call x0 -> x1, Pallas kernels: none -> 4.32 us  [restore(): pl.pallas_call(restore_kernel, grid=(RESTORE_STEPS,), out_shape=jax.Shape...]
    reshape x1 -> x0, local copies, waits for them, and re-layouts: 4.07 us -> none  [shards(): return result.reshape(columns_all, own, values).transpose(1, 0, 2)]
where the time goes in v4:
time: 120 us; the launch traced here: 119 us
  Pallas kernels  119 us (99%)
    pallas_call x1, Pallas kernels, assimilate(): pl.pallas_call(kernel, out_shape=jax.ShapeDtypeStruct((MEMBERS, columns,...  115 us
    pallas_call x1, Pallas kernels, restore(): pl.pallas_call(restore_kernel, grid=(RESTORE_STEPS,), out_shape=jax.Shape...  4.32 us

profile of v4, /device:TPU:1, one launch (start us, length us, event | category | flops | bytes accessed | tf_op | source)
XLA Modules:
  0.0 119.0 jit_solution(11530233307483275939)
XLA Ops:
  0.0 114.7 %shard_map.82.blocks_ref = bf16[8,16,16,512]{3,2,1,0:T(8,128)(2,1)} custom-call(s32[1,8,32,512]{3,2,1,0:T(8,128)} %send_ref.1, bf16[16,4096]{1,0:T(8,128)(2,1)} %obs_ref.1, f32[1,4096]{1,0:T(1,128)} %bitcast.8, f32[32,128]{1,0:T(8,128)} %bitcast.10, f32[32,128]{1,0:T(8,128)} %bitcast.9, s32[16,2048]{1,0:T(8,128)} %bitcast.6, s32[16,2048]{1,0:T(8,128)} %bitcast.7, ...), custom_call_target="tpu_custom_call" | custom-call | flops 20000000000 | bytes 12582912 | tf_op jit(solution)/shard_map/pallas_call | solution.py:461
  114.7 4.3 %shard_map.83 = bf16[16,128,512]{2,1,0:T(8,128)(2,1)} custom-call(bf16[8,16,16,512]{3,2,1,0:T(8,128)(2,1)} %shard_map.82.blocks_ref), custom_call_target="tpu_custom_call" | custom-call | tf_op jit(solution)/shard_map/pallas_call | solution.py:201

commit v5 on v4

--- a/solution.py
+++ b/solution.py
@@ -12,7 +12,7 @@
 LANES = 128
 CGROUP = 4
 OGROUP = 4
-RESTORE_STEPS = 4
+RESTORE_STEPS = 2
 MEMBERS = 8
 REGIONS = 32
 NZ = 8
@@ -348,9 +348,9 @@
         return 0
 
     build(0)
-    lax.fori_loop(0, 8, send, 0)
+    lax.fori_loop(0, 10, send, 0)
     forward(1)
-    lax.fori_loop(8, 16, send, 0)
+    lax.fori_loop(10, 16, send, 0)
     pair_dev_copy().wait_recv()
     pair_idx_copy().wait_recv()
     pair_smem = pltpu.make_async_copy(idx_ref.at[1], idx_smem.at[1], idx_sem.at[0])

time: 120 us -> 119 us (level)
    pallas_call x1, Pallas kernels: 4.32 us -> 3.1 us  [restore(): pl.pallas_call(restore_kernel, grid=(RESTORE_STEPS,), out_shape=jax.Shape...]
where the time goes in v5:
time: 119 us; the launch traced here: 118 us
  Pallas kernels  118 us (99%)
    pallas_call x1, Pallas kernels, assimilate(): pl.pallas_call(kernel, out_shape=jax.ShapeDtypeStruct((MEMBERS, columns,...  115 us
    pallas_call x1, Pallas kernels, restore(): pl.pallas_call(restore_kernel, grid=(RESTORE_STEPS,), out_shape=jax.Shape...  3.1 us

profile of v5, /device:TPU:1, one launch (start us, length us, event | category | flops | bytes accessed | tf_op | source)
XLA Modules:
  0.0 117.7 jit_solution(10916489942705336468)
XLA Ops:
  0.0 114.6 %shard_map.82.blocks_ref = bf16[8,16,16,512]{3,2,1,0:T(8,128)(2,1)} custom-call(s32[1,8,32,512]{3,2,1,0:T(8,128)} %send_ref.1, bf16[16,4096]{1,0:T(8,128)(2,1)} %obs_ref.1, f32[1,4096]{1,0:T(1,128)} %bitcast.8, f32[32,128]{1,0:T(8,128)} %bitcast.10, f32[32,128]{1,0:T(8,128)} %bitcast.9, s32[16,2048]{1,0:T(8,128)} %bitcast.6, s32[16,2048]{1,0:T(8,128)} %bitcast.7, ...), custom_call_target="tpu_custom_call" | custom-call | flops 20000000000 | bytes 12582912 | tf_op jit(solution)/shard_map/pallas_call | solution.py:461
  114.6 3.1 %shard_map.83 = bf16[16,128,512]{2,1,0:T(8,128)(2,1)} custom-call(bf16[8,16,16,512]{3,2,1,0:T(8,128)(2,1)} %shard_map.82.blocks_ref), custom_call_target="tpu_custom_call" | custom-call | tf_op jit(solution)/shard_map/pallas_call | solution.py:201

commit v6 on v5

--- a/solution.py
+++ b/solution.py
@@ -11,7 +11,7 @@
 NS_ITERS = 6
 LANES = 128
 CGROUP = 4
-OGROUP = 4
+OGROUP = 2
 RESTORE_STEPS = 2
 MEMBERS = 8
 REGIONS = 32
@@ -95,17 +95,14 @@
         right[0:K, lanes] = block
         right[K : K + 16, lanes] = jnp.where(first, dev, 0.0).astype(jnp.bfloat16)
         values.append(block.astype(jnp.float32))
-    for c in range(0, columns, 2):
-        weighted = []
-        for column in (c, c + 1):
-            pieces = []
-            for v, (r, block, dev) in zip(values, parts):
-                for q in range(lead):
-                    w = wmat[column, pl.ds(r * lead + q, 1), :]
-                    pieces.append((v[:, q * LANES : (q + 1) * LANES] * w).astype(jnp.bfloat16))
-            weighted.append(jnp.concatenate(pieces, axis=1))
-        acc[:, c * K : (c + 2) * K] += lax.dot_general(
-            right[...], jnp.concatenate(weighted, axis=0), NT, preferred_element_type=jnp.float32
+    for c in range(columns):
+        pieces = []
+        for v, (r, block, dev) in zip(values, parts):
+            for q in range(lead):
+                w = wmat[c, pl.ds(r * lead + q, 1), :]
+                pieces.append((v[:, q * LANES : (q + 1) * LANES] * w).astype(jnp.bfloat16))
+        acc[:, c * K : (c + 1) * K] += lax.dot_general(
+            right[...], jnp.concatenate(pieces, axis=1), NT, preferred_element_type=jnp.float32
         )
 
 

time: 119 us -> 119 us (level)
  no operation moved by 1% of the time
where the time goes in v6:
time: 119 us; the launch traced here: 118 us
  Pallas kernels  118 us (99%)
    pallas_call x1, Pallas kernels, assimilate(): pl.pallas_call(kernel, out_shape=jax.ShapeDtypeStruct((MEMBERS, columns,...  115 us
    pallas_call x1, Pallas kernels, restore(): pl.pallas_call(restore_kernel, grid=(RESTORE_STEPS,), out_shape=jax.Shape...  3.1 us

profile of v6, /device:TPU:1, one launch (start us, length us, event | category | flops | bytes accessed | tf_op | source)
XLA Modules:
  0.0 118.1 jit_solution(10735011810632590891)
XLA Ops:
  0.0 115.0 %shard_map.82.blocks_ref = bf16[8,16,16,512]{3,2,1,0:T(8,128)(2,1)} custom-call(s32[1,8,32,512]{3,2,1,0:T(8,128)} %send_ref.1, bf16[16,4096]{1,0:T(8,128)(2,1)} %obs_ref.1, f32[1,4096]{1,0:T(1,128)} %bitcast.8, f32[32,128]{1,0:T(8,128)} %bitcast.10, f32[32,128]{1,0:T(8,128)} %bitcast.9, s32[16,2048]{1,0:T(8,128)} %bitcast.6, s32[16,2048]{1,0:T(8,128)} %bitcast.7, ...), custom_call_target="tpu_custom_call" | custom-call | flops 20000000000 | bytes 12582912 | tf_op jit(solution)/shard_map/pallas_call | solution.py:458
  115.0 3.1 %shard_map.83 = bf16[16,128,512]{2,1,0:T(8,128)(2,1)} custom-call(bf16[8,16,16,512]{3,2,1,0:T(8,128)(2,1)} %shard_map.82.blocks_ref), custom_call_target="tpu_custom_call" | custom-call | tf_op jit(solution)/shard_map/pallas_call | solution.py:198
